TPU v7x, 32 devices: a whole 2x2x4 slice. The times are simulated.
32 devices in a mesh: groups: 2 (over x), tensor: 8 (over z, y), dp: 2 (over core).
Axes of the slice: x: 2, y: 2, z: 4, core: 2. Of those that a mesh axis runs over, the one named last changes fastest.
Arguments:
- hidden_act: bfloat16 [1536, 28672], P(('groups', 'dp'), 'tensor'), parts along dimension 0, may hold values from -6 to 6
- down_weight: bfloat16 [28672, 8192], P('tensor', 'dp'), may hold values from -0.046875 to 0.046875
- residual: bfloat16 [1536, 8192], P(('groups', 'dp'), 'tensor'), parts along dimension 0, may hold values from -6 to 6
- tap_early: bfloat16 [1536, 8192], P(('groups', 'dp'), 'tensor'), parts along dimension 0, may hold values from -6 to 6
- tap_middle: bfloat16 [1536, 8192], P(('groups', 'dp'), 'tensor'), parts along dimension 0, may hold values from -6 to 6
- merge_weight: bfloat16 [3, 8192, 5120], P(None, 'tensor', 'dp'), may hold values from -0.0546875 to 0.0546875
- q_gain: float32 [128], replicated, may hold values from 0.5 to 2
- k_gain: float32 [128], replicated, may hold values from 0.5 to 2
- lengths: int32 [4, 16], P(('groups', 'dp')), parts along dimension 0, may hold values from 1 to 93
- offsets: int32 [4, 16], P(('groups', 'dp')), parts along dimension 0, may hold values from 0 to 383, as said below
- owner_map: int32 [4, 16], P(('groups', 'dp')), parts along dimension 0, may hold values from 0 to 7, as said below
- loss_mask: int32 [1536], P(('groups', 'dp')), parts along dimension 0, may hold values 0 or 1
Outputs:
- draft_out: bfloat16 [3008, 4096], P(('groups', 'tensor', 'dp')), parts along dimension 0
There are 2 independent parts, one for each index of `groups`. A program takes and returns all parts, laid end to end along the dimension named above; an argument that names none is the same for every part. Nothing has to cross between parts.
Inputs may be any that keep to these rules, and one draw needn't show every extreme that they name: `owner_map`: in each data row every owner holds exactly two sequences, the sequences tile the row's 384 tokens in packing order, and the tokens of one row mapped to one owner number at most 94, reached by some owner in every row. offsets are the running sums of lengths in packing order.
All inputs are finite; a program needn't handle non-finite values. No bound on the sum of `loss_mask` on one device may be relied on, other than what follows from the above.
Results may differ from a plain program's by a relative error of at most 0.03.
Values may be sent and summed in bfloat16 or wider, within the bound.
A program may use at most 256 MiB of HBM per device.

v0:
```python
import math

import jax
import jax.numpy as jnp
from jax import lax
from jax.sharding import PartitionSpec as P

QH = 32
KH = 4
HS = 128


def slot_map(lengths, offsets, owners, slot_owner, slot_pos):
    index = jnp.arange(lengths.shape[0], dtype=jnp.int32)
    earlier = (owners[None, :] == owners[:, None]) & (index[None, :] < index[:, None])
    base = jnp.sum(jnp.where(earlier, lengths[None, :], 0), axis=1)
    hit = (
        (owners[None, :] == slot_owner[:, None])
        & (base[None, :] <= slot_pos[:, None])
        & (slot_pos[:, None] < (base + lengths)[None, :])
    )
    live = jnp.any(hit, axis=1)
    token = jnp.sum(jnp.where(hit, (offsets - base)[None, :] + slot_pos[:, None], 0), axis=1)
    sequence = jnp.where(live, jnp.sum(jnp.where(hit, index[None, :], 0), axis=1), -1)
    return (token, live, sequence)


def attend(merged, live, sequence, keep, q_gain, k_gain):
    slots = merged.shape[0]
    query = merged[:, : QH * HS].astype(jnp.float32).reshape(slots, KH, QH // KH, HS)
    keys = merged[:, QH * HS : (QH + KH) * HS].astype(jnp.float32).reshape(slots, KH, HS)
    values = merged[:, (QH + KH) * HS :].reshape(slots, KH, HS)
    query = query * lax.rsqrt(jnp.mean(query * query, axis=-1, keepdims=True) + 1e-06) * q_gain
    keys = keys * lax.rsqrt(jnp.mean(keys * keys, axis=-1, keepdims=True) + 1e-06) * k_gain
    scores = jnp.einsum("qkgd,skd->kgqs", query, keys) / math.sqrt(HS)
    place = jnp.arange(slots, dtype=jnp.int32)
    allowed = (
        (sequence[:, None] == sequence[None, :])
        & live[None, :]
        & (place[None, :] <= place[:, None])
    )
    scores = jnp.where(allowed, scores, -1e30)
    top = jnp.max(scores, axis=-1, keepdims=True)
    expo = jnp.exp(scores - top)
    weights = (expo / jnp.sum(expo, axis=-1, keepdims=True)).astype(jnp.bfloat16)
    result = jnp.einsum("kgqs,skd->qkgd", weights, values, preferred_element_type=jnp.float32)
    result = result.reshape(slots, QH * HS) * keep[:, None].astype(jnp.float32)
    return result.astype(jnp.bfloat16)


def local(
    hidden_act,
    down_weight,
    residual,
    tap_early,
    tap_middle,
    merge_weight,
    q_gain,
    k_gain,
    lengths,
    offsets,
    owner_map,
    loss_mask,
):
    tok_rows = hidden_act.shape[0]
    owners = lax.axis_size("tensor")
    capacity = 2 * tok_rows // owners - 2
    partial_sum = jnp.dot(
        hidden_act,
        lax.all_gather(down_weight, "dp", axis=1, tiled=True),
        preferred_element_type=jnp.float32,
    )
    summed = lax.psum_scatter(
        partial_sum.astype(jnp.bfloat16), "tensor", scatter_dimension=1, tiled=True
    ).astype(jnp.float32)
    tap_late = (residual.astype(jnp.float32) + summed).astype(jnp.bfloat16)
    stacked = jnp.stack([tap_early, tap_middle, tap_late], axis=1)
    every_slot = jnp.arange(owners * capacity, dtype=jnp.int32)
    send_token, send_live, unused = slot_map(
        lengths[0], offsets[0], owner_map[0], every_slot // capacity, every_slot % capacity
    )
    bucket = jnp.where(send_live[:, None, None], stacked[send_token], jnp.zeros((), jnp.bfloat16))
    whole_weight = lax.all_gather(merge_weight, "dp", axis=2, tiled=True)
    merged = lax.psum_scatter(
        jnp.einsum("ntd,tdc->nc", bucket, whole_weight, preferred_element_type=jnp.float32).astype(
            jnp.bfloat16
        ),
        "tensor",
        scatter_dimension=0,
        tiled=True,
    )
    own_slot = jnp.arange(capacity, dtype=jnp.int32)
    me_owner = jnp.zeros((capacity,), jnp.int32) + lax.axis_index("tensor")
    own_token, own_live, own_sequence = slot_map(
        lengths[0], offsets[0], owner_map[0], me_owner, own_slot
    )
    keep = own_live & (loss_mask[own_token] == 1)
    return attend(merged, own_live, own_sequence, keep, q_gain, k_gain)


def solution(mesh):
    return jax.shard_map(
        local,
        mesh=mesh,
        in_specs=(
            P(("groups", "dp"), "tensor"),
            P("tensor", "dp"),
            P(("groups", "dp"), "tensor"),
            P(("groups", "dp"), "tensor"),
            P(("groups", "dp"), "tensor"),
            P(None, "tensor", "dp"),
            P(),
            P(),
            P(("groups", "dp"), None),
            P(("groups", "dp"), None),
            P(("groups", "dp"), None),
            P(("groups", "dp")),
        ),
        out_specs=P(("groups", "tensor", "dp"), None),
        check_vma=False,
    )
```

profile of v0, /device:TPU:14, one launch (start us, length us, event | category | flops | bytes accessed | tf_op | source)
XLA Modules:
  0.0 598.4 jit_solution(12696099438677087259)
XLA Ops:
  6.5 0.0 copy-start
  6.5 0.0 all-gather.3.cloned.1.call-start
  6.5 0.7 all-gather.3.cloned.1.call-update
  7.3 0.0 reduce-scatter.2.cloned.1.call-start
  7.3 87.1 %all-gather.3.cloned.1.call-done = bf16[3584,8192]{1,0:T(8,128)(2,1)} async-done(((bf16[3584,4096]{1,0:T(8,128)(2,1)}), bf16[3584,8192]{1,0:T(8,128)(2,1)}) %all-gather.3.cloned.1.call-update) | async-done | bytes 58720272 | tf_op jit(solution)/shard_map/all_gather | solution.py:70
  94.4 0.0 copy-done
  94.4 29.7 %convolution_convert_fusion = bf16[384,8192]{1,0:T(8,128)(2,1)} fusion(bf16[384,3584]{1,0:T(8,128)(2,1)S(1)} %copy-done, bf16[3584,8192]{1,0:T(8,128)(2,1)} %all-gather.3.cloned.1.call-done), kind=kOutput, calls=%fused_computation.4 | convolution fusion | flops 22551724032 | bytes 67764224 | tf_op jit(solution)/shard_map/dot_general | solution.py:68
  124.2 0.0 reduce-scatter.2.cloned.1.call-update
  124.2 0.0 copy-start.6
  124.2 0.0 copy-start.7
  124.2 0.0 copy-start.9
  124.2 0.0 copy-start.5
  124.2 0.0 all-gather.5.cloned.1.call-start
  124.3 0.7 all-gather.5.cloned.1.call-update
  125.0 0.0 copy-start.3
  125.0 0.0 copy-start.4
  125.0 0.2 all-reduce.3.cloned.1.call-start
  125.2 0.0 copy-done.6
  125.2 0.0 copy-done.7
  125.3 0.2 select_reduce_fusion.3
  125.4 0.0 copy-done.9
  125.5 0.1 select_reduce_fusion
  125.6 0.1 fusion.30
  125.7 117.2 %reduce-scatter.2.cloned.1.call-done = bf16[384,1024]{1,0:T(8,128)(2,1)} async-done(((bf16[384,8192]{1,0:T(8,128)(2,1)}), bf16[384,1024]{1,0:T(8,128)(2,1)}) %reduce-scatter.2.cloned.1.call-update) | async-done | bytes 786448 | tf_op jit(solution)/shard_map/reduce_scatter | solution.py:73
  242.9 0.0 copy-done.5
  242.9 1.4 fusion.10
  244.3 0.0 copy-done.3
  244.3 0.0 copy-done.4
  244.3 0.3 pad_maximum_fusion
  244.6 2.0 copy.44
  246.6 20.7 %gather_fusion = bf16[752,3,1024]{2,1,0:T(4,128)(2,1)} fusion(bf16[384,3,1024]{2,1,0:T(4,128)(2,1)S(1)} %copy.44, s32[1024]{0:T(1024)S(1)} %pad_clamp_fusion.1), kind=kCustom, calls=%fused_computation | custom fusion | bytes 9243584 | tf_op jit(solution)/shard_map/gather | solution.py:82
  267.3 9.3 %broadcast_select_fusion = bf16[752,3,1024]{2,1,0:T(4,128)(2,1)} fusion(bf16[752,3,1024]{2,1,0:T(4,128)(2,1)} %gather_fusion, pred[752]{0:T(1024)(128)(4,1)S(1)} %fusion.30), kind=kLoop, calls=%fused_computation.5 | loop fusion | flops 2310144 | bytes 9241328 | tf_op jit(solution)/shard_map/jit(_where)/select_n | solution.py:82
  276.7 16.8 %all-gather.5.cloned.1.call-done = bf16[3,1024,5120]{2,1,0:T(8,128)(2,1)} async-done(((bf16[3,1024,2560]{2,1,0:T(8,128)(2,1)}), bf16[3,1024,5120]{2,1,0:T(8,128)(2,1)}) %all-gather.5.cloned.1.call-update) | async-done | bytes 31457296 | tf_op jit(solution)/shard_map/all_gather | solution.py:83
  293.5 37.3 %bitcast_convert_fusion = bf16[752,5120]{1,0:T(8,128)(2,1)} fusion(bf16[3,1024,5120]{2,1,0:T(8,128)(2,1)} %all-gather.5.cloned.1.call-done, bf16[752,3,1024]{2,1,0:T(4,128)(2,1)} %broadcast_select_fusion), kind=kOutput, calls=%fused_computation.3 | convolution fusion | flops 23659724800 | bytes 43778048 | tf_op jit(solution)/shard_map/ntd,tdc->nc/dot_general | solution.py:85
  330.7 0.0 all-reduce.3.cloned.1.call-update
  330.7 0.6 copy-done.11
  331.4 0.6 dynamic-slice
  332.6 0.1 select_reduce_fusion.1
  332.7 0.0 copy-done.2
  332.7 1.5 gather_fusion.1
  334.3 0.1 fusion.29
  334.4 0.1 fusion.13
  334.5 247.7 %all-reduce.3.cloned.1.call-done = bf16[752,5120]{1,0:T(8,128)(2,1)} async-done(((bf16[752,5120]{1,0:T(8,128)(2,1)}), bf16[752,5120]{1,0:T(8,128)(2,1)}) %all-reduce.3.cloned.1.call-update) | async-done | bytes 7700496
  582.2 1.3 dynamic-slice_convert_fusion
  583.6 0.3 copy.62
  583.9 0.0 copy-start.8
  583.9 0.0 copy-start.10
  583.9 1.1 fusion.31
  585.1 0.1 reshape.114
  585.1 0.2 multiply_reduce_fusion
  585.3 0.6 fusion.5
  586.0 0.1 copy.48
  586.1 0.2 copy.49
  586.2 0.0 copy-done.8
  586.2 0.2 multiply_bitcast_fusion
  586.4 0.5 fusion.6
  586.9 0.7 bitcast_select_fusion
  587.7 0.4 fusion.32
  588.1 0.6 convolution_bitcast_fusion
  588.7 0.9 copy.76
  589.6 0.1 pad.5
  589.7 0.0 copy-start.1
  589.7 1.1 copy.63
  590.8 1.1 multiply_convert_fusion
  (16 shorter events, 0.1 us)
Async XLA Ops:
  6.5 87.9 %copy-start = (bf16[384,3584]{1,0:T(8,128)(2,1)S(1)}, bf16[384,3584]{1,0:T(8,128)(2,1)}, u32[]{:S(2)}) copy-start(bf16[384,3584]{1,0:T(8,128)(2,1)} %param.12) | copy-start | bytes 8257540
  6.5 87.9 %all-gather.3.cloned.1.call-start = ((), (), s32[]{:S(2)}) async-start(), calls=%async_computation.1 | async-start | bytes 88080384 | tf_op jit(solution)/shard_map/all_gather | solution.py:70
  7.3 235.6 %reduce-scatter.2.cloned.1.call-start = ((), (), s32[]{:S(2)}) async-start(), calls=%async_computation.2 | async-start | bytes 7077888 | tf_op jit(solution)/shard_map/reduce_scatter | solution.py:73
  124.2 1.1 copy-start.6
  124.2 1.1 copy-start.7
  124.2 1.2 copy-start.9
  124.2 118.7 %copy-start.5 = (bf16[384,1024]{1,0:T(8,128)(2,1)S(1)}, bf16[384,1024]{1,0:T(8,128)(2,1)}, u32[]{:S(2)}) copy-start(bf16[384,1024]{1,0:T(8,128)(2,1)} %param.14) | copy-start | bytes 2359300
  124.2 169.2 %all-gather.5.cloned.1.call-start = ((), (), s32[]{:S(2)}) async-start(), calls=%async_computation.3 | async-start | bytes 47185920 | tf_op jit(solution)/shard_map/all_gather | solution.py:83
  125.0 119.3 %copy-start.3 = (bf16[384,1024]{1,0:T(8,128)(2,1)S(1)}, bf16[384,1024]{1,0:T(8,128)(2,1)}, u32[]{:S(2)}) copy-start(bf16[384,1024]{1,0:T(8,128)(2,1)} %param.16) | copy-start | bytes 2359300
  125.0 119.3 %copy-start.4 = (bf16[384,1024]{1,0:T(8,128)(2,1)S(1)}, bf16[384,1024]{1,0:T(8,128)(2,1)}, u32[]{:S(2)}) copy-start(bf16[384,1024]{1,0:T(8,128)(2,1)} %param.15) | copy-start | bytes 2359300
  125.0 457.2 %all-reduce.3.cloned.1.call-start = ((), (), s32[]{:S(2)}) async-start(), calls=%async_computation.4 | async-start | bytes 15400960
  330.7 0.7 copy-start.11
  330.7 2.0 copy-start.2
  583.9 2.4 copy-start.8
  583.9 2.5 copy-start.10
  589.7 2.2 copy-start.1
Sparse Core Ops, SparseCore 0:
  8.9 85.4 all-gather.2
  124.3 118.5 reduce-scatter.1
  244.4 48.9 all-gather.4
  330.9 251.3 all-reduce.2
where the time goes:
time: 602 us; the launch traced here: 598 us
  waiting for transfers between devices  470 us (78%)
  matrix products  68.3 us (11%)
  local copies, waits for them, and re-layouts  28.3 us (5%)
  other arithmetic  17.2 us (3%)
  between operations  14.1 us (2%)
    unnamed x5, waiting for transfers between devices  249 us
    reduce_scatter x1, waiting for transfers between devices, local(): lax.psum_scatter(partial_sum.astype(jnp.bfloat16), 'tensor', scatter_dime...  117 us
    all_gather x1, waiting for transfers between devices, local(): lax.all_gather(down_weight, 'dp', axis=1, tiled=True)  87.1 us
    dot_general x1, matrix products, local(): jnp.einsum('ntd,tdc->nc', bucket, whole_weight, preferred_element_type=jn...  37.3 us
    dot_general x1, matrix products, local(): jnp.dot(hidden_act, lax.all_gather(down_weight, 'dp', axis=1, tiled=True)...  29.7 us
    gather x1, local copies, waits for them, and re-layouts, local(): stacked[send_token]  20.7 us
    all_gather x1, waiting for transfers between devices, local(): whole_weight = lax.all_gather(merge_weight, 'dp', axis=2, tiled=True)  16.8 us
  transfers between devices with their start and end apart: 4, of which 4 were waited for; matrix products, arithmetic and copies ran while one was open for 6% of the time, Pallas kernels for 0%

commit v1 on v0

v1 whole, which is shorter than its diff:
```python
import math

import jax
import jax.numpy as jnp
from jax import lax
from jax.sharding import PartitionSpec as P

QH = 32
KH = 4
HS = 128
BF = jnp.bfloat16
F32 = jnp.float32


def swap(x):
    return lax.ppermute(x, "dp", [(0, 1), (1, 0)])


def head_order(per_core, core):
    order = []
    group = QH // KH
    for k in range(KH):
        for g in range(group // (2 * per_core)):
            first = k * group + g * 2 * per_core + core * per_core
            order += list(range(first, first + per_core))
            order.append(QH + core * KH + k)
    return order


def columns(x, blocks):
    return jnp.concatenate([x[..., b * HS : (b + 1) * HS] for b in blocks], axis=-1)


def own_columns(weight, core, per_core):
    half = weight.shape[-1] // HS
    need = [sorted(set(head_order(per_core, c))) for c in (0, 1)]
    send = [[b - c * half for b in need[1 - c] if b // half == c] for c in (0, 1)]
    sent = jnp.where(core == 0, columns(weight, send[0]), columns(weight, send[1]))
    came = swap(sent)
    both = jnp.concatenate([weight, came], axis=-1)

    def arranged(c):
        place = {b: b - c * half for b in need[c] if b // half == c}
        place.update({b + (1 - c) * half: half + i for i, b in enumerate(send[1 - c])})
        return columns(both, [place[b] for b in head_order(per_core, c)])

    return jnp.where(core == 0, arranged(0), arranged(1))


def norm(x, gain):
    return x * lax.rsqrt(jnp.mean(x * x, axis=-1, keepdims=True) + 1e-06) * gain


def attend(query, key, value, sequence, keep, q_gain, k_gain):
    tokens, wide = query.shape
    query = norm(query.astype(F32).reshape(tokens, wide // HS, HS), q_gain)
    key = norm(key.astype(F32), k_gain)
    scores = jnp.einsum("qhd,sd->hqs", query, key) / math.sqrt(HS)
    place = jnp.arange(tokens, dtype=jnp.int32)
    allowed = (sequence[:, None] == sequence[None, :]) & (place[None, :] <= place[:, None])
    scores = jnp.where(allowed, scores, -1e30)
    expo = jnp.exp(scores - jnp.max(scores, axis=-1, keepdims=True))
    weights = (expo / jnp.sum(expo, axis=-1, keepdims=True)).astype(BF)
    result = jnp.einsum("hqs,sd->qhd", weights, value, preferred_element_type=F32)
    return (result.reshape(tokens, wide) * keep[:, None]).astype(BF)


def local(
    hidden_act,
    down_weight,
    residual,
    tap_early,
    tap_middle,
    merge_weight,
    q_gain,
    k_gain,
    lengths,
    offsets,
    owner_map,
    loss_mask,
):
    rows = hidden_act.shape[0]
    chips = lax.axis_size("tensor")
    capacity = 2 * rows // chips - 2
    core = lax.axis_index("dp")
    chip = lax.axis_index("tensor")
    per_core = QH // chips
    wide = (per_core + 1) * HS
    n_seq = lengths.shape[1]

    hidden = lax.all_gather(hidden_act, "dp", axis=0, tiled=True)
    table = jnp.concatenate([lengths[0], offsets[0], owner_map[0], loss_mask])
    tables = lax.all_gather(table, "dp", axis=0, tiled=False)
    taps = lax.all_gather(jnp.concatenate([tap_early, tap_middle], axis=1), "dp", axis=0, tiled=True)

    partial_sum = jnp.dot(hidden, down_weight, preferred_element_type=F32).astype(BF)
    partial_sum = lax.all_to_all(partial_sum, "dp", split_axis=0, concat_axis=1, tiled=True)
    summed = lax.psum_scatter(partial_sum, "tensor", scatter_dimension=1, tiled=True).astype(F32)
    tap_late = (residual.astype(F32) + summed).astype(BF)
    late = lax.all_gather(tap_late, "dp", axis=0, tiled=True)

    weight = own_columns(merge_weight, core, per_core)
    joined = jnp.dot(taps, weight[:2].reshape(-1, weight.shape[2]), preferred_element_type=F32)
    joined = (joined + jnp.dot(late, weight[2], preferred_element_type=F32)).astype(BF)
    joined = joined.reshape(2, rows, chips // 2, wide).transpose(2, 0, 1, 3)
    merged = lax.psum_scatter(
        joined.reshape(chips, rows, wide), "tensor", scatter_dimension=0, tiled=False
    )

    row = chip % 2
    mine = jnp.where(row == 0, tables[0], tables[1])
    length, offset, owner = [mine[i * n_seq : (i + 1) * n_seq] for i in range(3)]
    keep = (mine[3 * n_seq :] == 1).astype(F32)
    token = jnp.arange(rows, dtype=jnp.int32)
    inside = (offset[None, :] <= token[:, None]) & (token[:, None] < (offset + length)[None, :])
    sequence = jnp.sum(jnp.where(inside, jnp.arange(n_seq, dtype=jnp.int32)[None, :], 0), axis=1)
    index = jnp.arange(n_seq, dtype=jnp.int32)
    earlier = (owner[None, :] == owner[:, None]) & (index[None, :] < index[:, None])
    base = jnp.sum(jnp.where(earlier, length[None, :], 0), axis=1)
    start = owner * capacity + base - offset
    slot = token + jnp.sum(jnp.where(inside, start[None, :], 0), axis=1)
    place = (jnp.arange(chips * capacity, dtype=jnp.int32)[:, None] == slot[None, :]).astype(BF)

    query, mine_kv = merged[:, : per_core * HS], merged[:, per_core * HS :]
    other_kv = swap(mine_kv)
    key = jnp.where(core == 0, mine_kv, other_kv)
    value = jnp.where(core == 0, other_kv, mine_kv)
    result = attend(query, key, value, sequence, keep, q_gain, k_gain)
    slots = jnp.dot(place, result, preferred_element_type=F32).astype(BF)
    slots = lax.all_to_all(
        slots.reshape(chips, capacity, per_core * HS), "tensor", split_axis=0, concat_axis=0, tiled=True
    )
    slots = slots.reshape(chips // 2, 2, capacity, per_core * HS)
    first, second = slots[:, 0], slots[:, 1]
    own = jnp.where(core == 0, first, second)
    came = swap(jnp.where(core == 0, second, first))
    low = jnp.where(core == 0, own, came)
    high = jnp.where(core == 0, came, own)
    out = jnp.stack([low, high], axis=1)
    return out.transpose(2, 0, 1, 3).reshape(capacity, QH * HS)


def solution(mesh):
    return jax.shard_map(
        local,
        mesh=mesh,
        in_specs=(
            P(("groups", "dp"), "tensor"),
            P("tensor", "dp"),
            P(("groups", "dp"), "tensor"),
            P(("groups", "dp"), "tensor"),
            P(("groups", "dp"), "tensor"),
            P(None, "tensor", "dp"),
            P(),
            P(),
            P(("groups", "dp"), None),
            P(("groups", "dp"), None),
            P(("groups", "dp"), None),
            P(("groups", "dp")),
        ),
        out_specs=P(("groups", "tensor", "dp"), None),
        check_vma=False,
    )
```

time: 602 us -> 421 us (0.70)
  waiting for transfers between devices: 470 us -> 211 us
  local copies, waits for them, and re-layouts: 28.3 us -> 75.3 us
  blocking collectives: 0 us -> 33.6 us
  matrix products: 68.3 us -> 58.1 us
  other arithmetic: 17.2 us -> 24 us
    unnamed x5, waiting for transfers between devices: 249 us -> 0.78 us
    all_gather x2 -> x3, waiting for transfers between devices: 104 us -> 18.6 us  [the longest x1 18.6 us: local(): hidden = lax.all_gather(hidden_act, 'dp', axis=0, tiled=True)]
    reduce_scatter x1 -> x2, waiting for transfers between devices: 117 us -> 190 us  [the longest x1 109 us: local(): lax.psum_scatter(partial_sum, 'tensor', scatter_dimension=1, tiled=True)]
    all_to_all x0 -> x2, blocking collectives: none -> 31.8 us  [the longest x1 23 us: local(): lax.all_to_all(slots.reshape(chips, capacity, per_core * HS), 'tensor', s...]
    unnamed x28 -> x40, local copies, waits for them, and re-layouts: 2.78 us -> 34.5 us
    gather x2 -> x0, local copies, waits for them, and re-layouts: 22.2 us -> none  [the longest x1 20.7 us: local(): stacked[send_token]]
    slice x0 -> x5, local copies, waits for them, and re-layouts: none -> 16.2 us  [the longest x1 8.62 us: local(): weight[:2].reshape(-1, weight.shape[2])]
    dot_general x4 -> x5, matrix products: 68.3 us -> 55.5 us  [the longest x1 28.1 us: local(): jnp.dot(hidden, down_weight, preferred_element_type=F32).astype(BF)]
  transfers between devices with their start and end apart: 4 -> 8, of which waited for: 4 -> 5; matrix products, arithmetic and copies ran while one was open for 6% -> 20% of each run, Pallas kernels for 0% -> 0%
where the time goes in v1:
time: 421 us; the launch traced here: 417 us
  waiting for transfers between devices  211 us (50%)
  local copies, waits for them, and re-layouts  75.3 us (18%)
  matrix products  58.1 us (14%)
  blocking collectives  33.6 us (8%)
  other arithmetic  24 us (6%)
  between operations  14.1 us (3%)
    reduce_scatter x1, waiting for transfers between devices, local(): lax.psum_scatter(partial_sum, 'tensor', scatter_dimension=1, tiled=True)  109 us
    reduce_scatter x1, waiting for transfers between devices, local(): lax.psum_scatter(joined.reshape(chips, rows, wide), 'tensor', scatter_dim...  80.5 us
    unnamed x40, local copies, waits for them, and re-layouts  34.5 us
    dot_general x1, matrix products, local(): jnp.dot(hidden, down_weight, preferred_element_type=F32).astype(BF)  28.1 us
    all_to_all x1, blocking collectives, local(): lax.all_to_all(slots.reshape(chips, capacity, per_core * HS), 'tensor', s...  23 us
    all_gather x1, waiting for transfers between devices, local(): hidden = lax.all_gather(hidden_act, 'dp', axis=0, tiled=True)  18.6 us
    dot_general x1, matrix products, local(): jnp.dot(taps, weight[:2].reshape(-1, weight.shape[2]), preferred_element_...  14.4 us
    select_n x1, other arithmetic, own_columns(): return jnp.where(core == 0, arranged(0), arranged(1))  13.6 us
  transfers between devices with their start and end apart: 8, of which 5 were waited for; matrix products, arithmetic and copies ran while one was open for 20% of the time, Pallas kernels for 0%

profile of v1, /device:TPU:14, one launch (start us, length us, event | category | flops | bytes accessed | tf_op | source)
XLA Modules:
  0.0 416.5 jit_solution(9038438565003471638)
XLA Ops:
  6.5 0.7 all-gather.7.cloned.1.call-update
  7.3 0.0 reduce-scatter.3.cloned.1.call-start
  7.3 18.6 %all-gather.7.cloned.1.call-done = bf16[768,3584]{1,0:T(8,128)(2,1)} async-done(((bf16[384,3584]{1,0:T(8,128)(2,1)}), bf16[768,3584]{1,0:T(8,128)(2,1)}) %all-gather.7.cloned.1.call-update) | async-done | bytes 5505040 | tf_op jit(solution)/shard_map/all_gather | solution.py:91
  25.9 28.1 %convolution_convert_fusion = bf16[768,4096]{1,0:T(8,128)(2,1)S(1)} fusion(bf16[768,3584]{1,0:T(8,128)(2,1)} %all-gather.7.cloned.1.call-done, bf16[3584,4096]{1,0:T(8,128)(2,1)} %param.13), kind=kOutput, calls=%fused_computation.3 | convolution fusion | flops 22551724032 | bytes 41156608 | tf_op jit(solution)/shard_map/dot_general | solution.py:96
  54.0 8.8 %all_to_all.24 = bf16[2,384,4096]{2,1,0:T(8,128)(2,1)S(1)} all-to-all(bf16[2,384,4096]{2,1,0:T(8,128)(2,1)S(1)} %bitcast.111), channel_id=1, replica_groups=mesh['groups'=2,'tensor'=8,'dp'=2] {'dp'}, dimensions={0} | all-to-all | bytes 12582912 | tf_op jit(solution)/shard_map/all_to_all | solution.py:97
  62.7 3.1 copy.49
  65.8 0.0 all-gather.9.cloned.1.call-start
  65.9 5.6 %fusion.49 = (bf16[3,1024,512]{2,1,0:T(8,128)(2,1)S(1)}, bf16[3,1024,512]{2,1,0:T(8,128)(2,1)S(1)}, bf16[3,1024,2560]{2,1,0:T(8,128)(2,1)}) fusion(bf16[3,1024,2560]{2,1,0:T(8,128)(2,1)} %param.17), kind=kLoop, calls=%fused_computation.91 | loop fusion | bytes 18874368 | tf_op jit(solution)/shard_map/slice | solution.py:31
  71.5 3.7 pad_maximum_fusion
  75.1 0.1 collective-permute-start
  75.3 109.3 %reduce-scatter.3.cloned.1.call-done = bf16[384,1024]{1,0:T(8,128)(2,1)} async-done(((bf16[384,8192]{1,0:T(8,128)(2,1)}), bf16[384,1024]{1,0:T(8,128)(2,1)}) %reduce-scatter.3.cloned.1.call-update) | async-done | bytes 786448 | tf_op jit(solution)/shard_map/reduce_scatter | solution.py:98
  184.5 2.3 add_convert_fusion.1
  186.8 0.0 all-gather.9.cloned.1.call-update
  186.9 0.0 all-gather.5.cloned.1.call-start
  186.9 1.3 pad_maximum_fusion.1
  188.2 0.2 reduce-scatter.5.cloned.1.call-start
  188.5 4.0 slice_dynamic-update-slice_fusion.2
  192.5 2.4 slice_dynamic-update-slice_fusion.15
  194.9 4.2 %slice_dynamic-update-slice_fusion = bf16[3,1024,2560]{2,1,0:T(8,128)(2,1)} fusion(bf16[3,1024,2560]{2,1,0:T(8,128)(2,1)} %slice_dynamic-update-slice_fusion.15, bf16[3,1024,1024]{2,1,0:T(8,128)(2,1)} %collective-permute-done), kind=kLoop, calls=%fused_computation.7 | loop fusion | bytes 6291456
  199.0 2.3 slice_dynamic-update-slice_fusion.14
  201.3 2.2 slice_dynamic-update-slice_fusion.11
  203.5 7.0 %slice_dynamic-update-slice_fusion.6 = (bf16[3,1024,2560]{2,1,0:T(8,128)(2,1)}, bf16[3,1024,2560]{2,1,0:T(8,128)(2,1)}) fusion(bf16[3,1024,2560]{2,1,0:T(8,128)(2,1)} %slice_dynamic-update-slice_fusion.14, bf16[3,1024,2560]{2,1,0:T(8,128)(2,1)} %param.17, bf16[3,1024,2560]{2,1,0:T(8,128)(2,1)} %slice_dynamic-update-slice_fusion.11), kind=kLoop, calls=%fused_computation.13 | loop fusion | bytes 12582912
  210.5 2.6 slice_dynamic-update-slice_fusion.10
  213.0 3.4 slice_dynamic-update-slice_fusion.4
  216.4 1.1 slice_dynamic-update-slice_fusion.12
  217.5 2.1 slice_dynamic-update-slice_fusion.9
  219.6 3.8 slice_dynamic-update-slice_fusion.3
  223.5 2.1 slice_dynamic-update-slice_fusion.8
  225.6 13.6 %broadcast_select_fusion = bf16[3,1024,2560]{2,1,0:T(8,128)(2,1)} fusion(bf16[3,1024,2560]{2,1,0:T(8,128)(2,1)} %slice_dynamic-update-slice_fusion.8, bf16[3,1024,2560]{2,1,0:T(8,128)(2,1)} %slice_dynamic-update-slice_fusion.12, pred[]{:T(512)S(6)} %eq.29), kind=kLoop, calls=%fused_computation.1 | loop fusion | flops 7864320 | bytes 47185920 | tf_op jit(solution)/shard_map/jit(_where)/select_n | solution.py:47
  239.2 8.6 %slice.183 = bf16[2,1024,2560]{2,1,0:T(8,128)(2,1)} slice(bf16[3,1024,2560]{2,1,0:T(8,128)(2,1)} %broadcast_select_fusion), slice={[0:2], [0:1024], [0:2560]} | slice | bytes 20971520 | tf_op jit(solution)/shard_map/slice | solution.py:103
  247.8 10.3 %fusion.1 = f32[768,2560]{1,0:T(8,128)} fusion(bf16[768,1024]{1,0:T(8,128)(2,1)} %all-gather.9.cloned.1.call-done, bf16[3,1024,2560]{2,1,0:T(8,128)(2,1)} %broadcast_select_fusion), kind=kOutput, calls=%fused_computation.6 | convolution fusion | flops 4026531840 | bytes 14680064 | tf_op jit(solution)/shard_map/dot_general | solution.py:104
  258.1 14.4 %add_convert_fusion = bf16[768,2560]{1,0:T(8,128)(2,1)} fusion(f32[768,2560]{1,0:T(8,128)} %fusion.1, bf16[768,2048]{1,0:T(8,128)(2,1)} %all-gather.5.cloned.1.call-done, bf16[2048,2560]{1,0:T(8,128)(2,1)} %bitcast.108), kind=kOutput, calls=%fused_computation.2 | convolution fusion | flops 8056995840 | bytes 25427968 | tf_op jit(solution)/shard_map/dot_general | solution.py:103
  272.5 7.6 %reshape.80 = bf16[2,384,4,640]{3,2,1,0:T(4,128)(2,1)} reshape(bf16[768,2560]{1,0:T(8,128)(2,1)} %add_convert_fusion) | data formatting | bytes 7864320 | tf_op jit(solution)/shard_map/reshape | solution.py:105
  280.2 8.2 %copy.37 = bf16[4,2,384,640]{2,3,1,0:T(8,128)(2,1)} copy(bf16[4,2,384,640]{3,0,2,1:T(4,128)(2,1)} %bitcast.107) | data formatting | bytes 7864320 | tf_op jit(solution)/shard_map/transpose | solution.py:105
  288.4 0.6 dynamic-slice
  289.7 0.2 add_dynamic-update-slice_fusion
  289.9 1.8 all-reduce
  291.7 0.1 slice_select_fusion
  291.8 0.1 fusion.44
  291.9 0.1 slice_bitcast_fusion.6
  291.9 0.2 select_reduce_fusion.2
  292.1 0.1 fusion.47
  292.2 0.1 select_reduce_fusion.1
  292.3 0.1 fusion.11
  292.4 80.5 %reduce-scatter.5.cloned.1.call-done = bf16[1,384,640]{1,2,0:T(8,128)(2,1)} async-done(((bf16[8,384,640]{1,2,0:T(8,128)(2,1)}), bf16[1,384,640]{1,2,0:T(8,128)(2,1)}) %reduce-scatter.5.cloned.1.call-update) | async-done | bytes 491536 | tf_op jit(solution)/shard_map/reduce_scatter | solution.py:106
  373.0 0.9 slice.185
  373.9 1.1 multiply_reduce_fusion
  375.0 0.1 collective-permute-start.1
  375.0 1.0 slice.186
  376.1 0.2 copy.38
  376.3 0.1 collective-permute-done.1
  376.3 0.9 fusion.17
  377.3 2.6 fusion.50
  379.9 2.1 fusion.5
  382.0 0.1 fusion.7
  382.1 0.6 convolution_convert_fusion.1
  382.7 0.2 reshape.85
  382.9 23.0 %all_to_all.25 = bf16[8,94,512]{2,1,0:T(8,128)(2,1)S(1)} all-to-all(bf16[8,94,512]{2,1,0:T(8,128)(2,1)S(1)} %reshape.85), channel_id=1, replica_groups=mesh['groups'=2,'tensor'=8,'dp'=2] {'tensor'}, dimensions={0} | all-to-all | bytes 1540096 | tf_op jit(solution)/shard_map/all_to_all | solution.py:130
  405.9 0.1 collective-permute-start.2
  406.0 1.7 collective-permute-done.2
  407.7 0.1 fusion.13
  407.8 0.1 maximum_bitcast_fusion
  407.9 0.8 copy.43
  408.7 1.3 reshape.87
  (41 shorter events, 0.2 us)
Async XLA Ops:
  6.5 19.3 %all-gather.7.cloned.1.call-start = ((), (), s32[]{:S(2)}) async-start(), calls=%async_computation.5 | async-start | bytes 8257536 | tf_op jit(solution)/shard_map/all_gather | solution.py:91
  7.3 177.3 %reduce-scatter.3.cloned.1.call-start = ((), (), s32[]{:S(2)}) async-start(), calls=%async_computation.6 | async-start | bytes 7077888 | tf_op jit(solution)/shard_map/reduce_scatter | solution.py:98
  65.8 182.0 %all-gather.9.cloned.1.call-start = ((), (), s32[]{:S(2)}) async-start(), calls=%async_computation.7 | async-start | bytes 2359296 | tf_op jit(solution)/shard_map/all_gather | solution.py:100
  71.4 113.1 %copy-start = (bf16[384,1024]{1,0:T(8,128)(2,1)S(1)}, bf16[384,1024]{1,0:T(8,128)(2,1)}, u32[]{:S(2)}) copy-start(bf16[384,1024]{1,0:T(8,128)(2,1)} %param.14) | copy-start | bytes 2359300
  71.4 115.5 %copy-start.1 = (bf16[384,1024]{1,0:T(8,128)(2,1)S(1)}, bf16[384,1024]{1,0:T(8,128)(2,1)}, u32[]{:S(2)}) copy-start(bf16[384,1024]{1,0:T(8,128)(2,1)} %param.16) | copy-start | bytes 2359300
  71.5 115.5 %copy-start.2 = (bf16[384,1024]{1,0:T(8,128)(2,1)S(1)}, bf16[384,1024]{1,0:T(8,128)(2,1)}, u32[]{:S(2)}) copy-start(bf16[384,1024]{1,0:T(8,128)(2,1)} %param.15) | copy-start | bytes 2359300
  75.1 113.3 %collective-permute-start = (bf16[3,1024,1024]{2,1,0:T(8,128)(2,1)}, bf16[3,1024,1024]{2,1,0:T(8,128)(2,1)}, u32[]{:S(2)}, u32[]{:S(2)}) collective-permute-start(bf16[3,1024,1024]{2,1,0:T(8,128)(2,1)} %pad_maximum_fusion), channel_id=1, source_target_pairs={{0,1},{1,0},{2,3},{3,2},{4,5},{5,4},{6,7},{7,6},{8,9},{9,8},{10,11... | collective-permute-start | bytes 18874376 | tf_op jit(solution)/shard_map/ppermute | solution.py:16
  186.9 71.2 %all-gather.5.cloned.1.call-start = ((), (), s32[]{:S(2)}) async-start(), calls=%async_computation.4 | async-start | bytes 4718592 | tf_op jit(solution)/shard_map/all_gather | solution.py:94
  188.2 184.7 %reduce-scatter.5.cloned.1.call-start = ((), (), s32[]{:S(2)}) async-start(), calls=%async_computation.8 | async-start | bytes 4423680 | tf_op jit(solution)/shard_map/reduce_scatter | solution.py:106
  188.5 22.0 %slice-start = ((s8[15728640]{0:T(1024)(128)(4,1)}), s8[4194304]{0:T(1024)(128)(4,1)S(1)}, s32[]{:S(2)}) async-start(s8[15728640]{0:T(1024)(128)(4,1)} %bitcast.102), calls=%async_computation.9 | async-start | bytes 8388608
  192.5 17.9 %slice-start.1 = ((s8[15728640]{0:T(1024)(128)(4,1)}), s8[4194304]{0:T(1024)(128)(4,1)S(1)}, s32[]{:S(2)}) async-start(s8[15728640]{0:T(1024)(128)(4,1)} %bitcast.102), calls=%async_computation.10 | async-start | bytes 8388608
  199.0 11.4 %slice-start.2 = ((s8[15728640]{0:T(1024)(128)(4,1)}), s8[4194304]{0:T(1024)(128)(4,1)S(1)}, s32[]{:S(2)}) async-start(s8[15728640]{0:T(1024)(128)(4,1)} %bitcast.102), calls=%async_computation.11 | async-start | bytes 8388608
  203.5 7.0 %slice-start.3 = ((s8[15728640]{0:T(1024)(128)(4,1)}), s8[3145728]{0:T(1024)(128)(4,1)S(1)}, s32[]{:S(2)}) async-start(s8[15728640]{0:T(1024)(128)(4,1)} %bitcast.102), calls=%async_computation.12 | async-start | bytes 6291456
  280.1 8.3 %copy-start.9 = (u32[32]{0:T(128)S(1)}, u32[32]{0:T(128)}, u32[]{:S(2)}) copy-start(u32[32]{0:T(128)} %constant.47) | copy-start | bytes 388
  280.2 9.5 %copy-start.3 = (s32[384]{0:T(512)S(1)}, s32[384]{0:T(512)}, u32[]{:S(2)}) copy-start(s32[384]{0:T(512)} %param.23) | copy-start | bytes 4612
  280.2 9.5 %copy-start.4 = (s32[1,16]{1,0:T(1,128)S(1)}, s32[1,16]{1,0:T(1,128)}, u32[]{:S(2)}) copy-start(s32[1,16]{1,0:T(1,128)} %param.22) | copy-start | bytes 196
  280.2 9.5 %copy-start.5 = (s32[1,16]{1,0:T(1,128)S(1)}, s32[1,16]{1,0:T(1,128)}, u32[]{:S(2)}) copy-start(s32[1,16]{1,0:T(1,128)} %param.21) | copy-start | bytes 196
  280.2 9.5 %copy-start.6 = (s32[1,16]{1,0:T(1,128)S(1)}, s32[1,16]{1,0:T(1,128)}, u32[]{:S(2)}) copy-start(s32[1,16]{1,0:T(1,128)} %param.20) | copy-start | bytes 196
  280.2 97.1 %copy-start.7 = (f32[128]{0:T(128)S(1)}, f32[128]{0:T(128)}, u32[]{:S(2)}) copy-start(f32[128]{0:T(128)} %param.18) | copy-start | bytes 1540
  280.2 97.1 %copy-start.8 = (f32[128]{0:T(128)S(1)}, f32[128]{0:T(128)}, u32[]{:S(2)}) copy-start(f32[128]{0:T(128)} %param.19) | copy-start | bytes 1540
  375.0 1.4 collective-permute-start.1
  405.9 1.8 collective-permute-start.2
Sparse Core Ops, SparseCore 0:
  8.9 16.9 all-gather.6
  66.0 118.5 reduce-scatter.2
  187.0 9.9 all-gather.8
  198.4 13.2 all-gather.4
  288.5 84.3 reduce-scatter.4

commit v2 on v1

--- a/solution.py
+++ b/solution.py
@@ -3,6 +3,8 @@
 import jax
 import jax.numpy as jnp
 from jax import lax
+from jax.experimental import pallas as pl
+from jax.experimental.pallas import tpu as pltpu
 from jax.sharding import PartitionSpec as P
 
 QH = 32
@@ -10,6 +12,7 @@
 HS = 128
 BF = jnp.bfloat16
 F32 = jnp.float32
+MESH = pl.DeviceIdType.MESH
 
 
 def swap(x):
@@ -63,6 +66,425 @@
     weights = (expo / jnp.sum(expo, axis=-1, keepdims=True)).astype(BF)
     result = jnp.einsum("hqs,sd->qhd", weights, value, preferred_element_type=F32)
     return (result.reshape(tokens, wide) * keep[:, None]).astype(BF)
+
+
+TILE = 256
+
+
+def matmul(a, b):
+    return jnp.dot(a, b, preferred_element_type=F32)
+
+
+def greet(z, y, core):
+    barrier = pltpu.get_barrier_semaphore()
+    pl.semaphore_signal(barrier, 1, device_id={"tensor": z * 2 + 1 - y}, device_id_type=MESH)
+    pl.semaphore_signal(barrier, 1, device_id={"dp": 1 - core}, device_id_type=MESH)
+
+    @pl.when(z > 0)
+    def _():
+        pl.semaphore_signal(barrier, 1, device_id={"tensor": (z - 1) * 2 + y}, device_id_type=MESH)
+
+    @pl.when(z < 3)
+    def _():
+        pl.semaphore_signal(barrier, 1, device_id={"tensor": (z + 1) * 2 + y}, device_id_type=MESH)
+
+    pl.semaphore_wait(barrier, jnp.where((z == 0) | (z == 3), 3, 4))
+
+
+def reduce_units(count, z, y, dest, product, finish, yout, own, yin, zin, sems):
+    y_send, y_recv, z_send, z_recv = sems
+
+    def y_copy(u):
+        return pltpu.make_async_remote_copy(
+            yout.at[u], yin.at[u], y_send.at[u], y_recv.at[u],
+            device_id={"tensor": z * 2 + 1 - y}, device_id_type=MESH,
+        )
+
+    def z_copy(u, way):
+        target = (z + 1 + 2 * way) % 4
+        return pltpu.make_async_remote_copy(
+            own.at[u], zin.at[way, u], z_send.at[u], z_recv.at[way, u],
+            device_id={"tensor": target * 2 + y}, device_id_type=MESH,
+        )
+
+    def first(u, _):
+        yout[u] = product(u, 0).astype(BF)
+        y_copy(u).start()
+        return 0
+
+    lax.fori_loop(0, count, first, 0)
+
+    def pass_on(i, way, place, edge):
+        u = i - place
+
+        @pl.when((u >= 0) & (u < count))
+        def _():
+            ahead = dest(u) - z if way == 0 else z - dest(u)
+
+            @pl.when(ahead > 0)
+            def _():
+                y_copy(u).wait_recv()
+
+                @pl.when(z == edge)
+                def _():
+                    own[u] = (own[u].astype(F32) + yin[u].astype(F32)).astype(BF)
+
+                @pl.when(z != edge)
+                def _():
+                    z_copy(u, way).wait_recv()
+                    total = own[u].astype(F32) + yin[u].astype(F32) + zin[way, u].astype(F32)
+                    own[u] = total.astype(BF)
+
+                z_copy(u, way).start()
+
+    def second(i, _):
+        @pl.when(i < count)
+        def _():
+            own[i] = product(i, 1).astype(BF)
+
+        pass_on(i, 0, z, 0)
+        pass_on(i, 1, 3 - z, 3)
+        u = i - 3
+
+        @pl.when(u >= 0)
+        def _():
+            @pl.when(dest(u) == z)
+            def _():
+                y_copy(u).wait_recv()
+
+                @pl.when(z == 0)
+                def _():
+                    z_copy(u, 1).wait_recv()
+                    finish(u, own[u].astype(F32) + yin[u].astype(F32) + zin[1, u].astype(F32))
+
+                @pl.when(z == 3)
+                def _():
+                    z_copy(u, 0).wait_recv()
+                    finish(u, own[u].astype(F32) + yin[u].astype(F32) + zin[0, u].astype(F32))
+
+                @pl.when((z > 0) & (z < 3))
+                def _():
+                    z_copy(u, 0).wait_recv()
+                    z_copy(u, 1).wait_recv()
+                    total = own[u].astype(F32) + yin[u].astype(F32)
+                    finish(u, total + zin[0, u].astype(F32) + zin[1, u].astype(F32))
+
+        return 0
+
+    lax.fori_loop(0, count + 3, second, 0)
+
+    def last(u, _):
+        y_copy(u).wait_send()
+
+        @pl.when(dest(u) != z)
+        def _():
+            z_copy(u, 0).wait_send()
+
+        return 0
+
+    lax.fori_loop(0, count, last, 0)
+
+
+def down_kernel(
+    hidden_ref, weight_ref, residual_ref, early_ref, middle_ref, taps_ref,
+    hidden, weight, res, yout, own, yin, zin,
+    w_sem, in_sem, far_send, far_recv, y_send, y_recv, z_send, z_recv, out_send, out_recv,
+):
+    rows, width = residual_ref.shape
+    tiles = width // TILE
+    count = 4 * tiles
+    chip, core = lax.axis_index("tensor"), lax.axis_index("dp")
+    z, y = chip // 2, chip % 2
+    other = {"dp": 1 - core}
+    mine = pl.ds(pl.multiple_of(core * rows, rows), rows)
+
+    def fetch(s):
+        u, stage = s % count, s // count
+        block = 2 * (u % 2) + (1 - y) * (1 - stage) + y * stage
+        column = block * width + (u // 2) % tiles * TILE
+        source = weight_ref.at[:, pl.ds(pl.multiple_of(column, TILE), TILE)]
+        return pltpu.make_async_copy(source, weight.at[s % 2], w_sem.at[s % 2])
+
+    near = [
+        pltpu.make_async_copy(hidden_ref, hidden.at[0], in_sem.at[0]),
+        pltpu.make_async_copy(residual_ref, res.at[0], in_sem.at[1]),
+        pltpu.make_async_copy(early_ref, taps_ref.at[0, mine], in_sem.at[2]),
+        pltpu.make_async_copy(middle_ref, taps_ref.at[1, mine], in_sem.at[3]),
+    ]
+    near[0].start()
+    fetch(0).start()
+    greet(z, y, core)
+    pairs = [
+        (hidden_ref, hidden.at[1]),
+        (residual_ref, res.at[1]),
+        (early_ref, taps_ref.at[0, mine]),
+        (middle_ref, taps_ref.at[1, mine]),
+    ]
+    far = [
+        pltpu.make_async_remote_copy(
+            a, b, far_send.at[i], far_recv.at[i], device_id=other, device_id_type=MESH
+        )
+        for i, (a, b) in enumerate(pairs)
+    ]
+    far[0].start()
+    for copy in near[1:]:
+        copy.start()
+    near[0].wait()
+    for copy in far[1:]:
+        copy.start()
+
+    def product(u, stage):
+        s = stage * count + u
+
+        @pl.when(s == count // 2)
+        def _():
+            far[0].wait_recv()
+
+        fetch(s).wait()
+
+        @pl.when(s + 1 < 2 * count)
+        def _():
+            fetch(s + 1).start()
+
+        return matmul(hidden[u // (count // 2)], weight[s % 2])
+
+    def out_copy(u, source_core):
+        half = (source_core + u // (count // 2)) % 2
+        place = taps_ref.at[
+            2,
+            pl.ds(pl.multiple_of(half * rows, rows), rows),
+            pl.ds(pl.multiple_of((u // 2) % tiles * TILE, TILE), TILE),
+        ]
+        return pltpu.make_async_remote_copy(
+            place, place, out_send.at[u // 2], out_recv.at[u // 2], device_id=other, device_id_type=MESH
+        )
+
+    near[1].wait()
+    far[1].wait_recv()
+
+    def finish(u, total):
+        half = (core + u // (count // 2)) % 2
+        column = pl.ds(pl.multiple_of((u // 2) % tiles * TILE, TILE), TILE)
+        late = total + res[u // (count // 2), :, column].astype(F32)
+        taps_ref[2, pl.ds(pl.multiple_of(half * rows, rows), rows), column] = late.astype(BF)
+        out_copy(u, core).start()
+
+    sems = (y_send, y_recv, z_send, z_recv)
+    reduce_units(
+        count, z, y, lambda u: 2 * core + u % 2, product, finish, yout, own, yin, zin, sems
+    )
+
+    def close(r, _):
+        @pl.when(z // 2 == core)
+        def _():
+            out_copy(2 * r, core).wait_send()
+
+        @pl.when(z // 2 != core)
+        def _():
+            out_copy(2 * r, 1 - core).wait_recv()
+
+        return 0
+
+    lax.fori_loop(0, count // 2, close, 0)
+    for copy in near[2:]:
+        copy.wait()
+    for copy in far:
+        copy.wait_send()
+    for copy in far[2:]:
+        copy.wait_recv()
+
+
+def join_kernel(
+    taps_ref, weight_ref, merged_ref,
+    weight, yout, own, yin, zin,
+    w_sem, y_send, y_recv, z_send, z_recv, out_send, out_recv,
+):
+    rows = merged_ref.shape[1]
+    count = weight_ref.shape[2] // TILE
+    chip, core = lax.axis_index("tensor"), lax.axis_index("dp")
+    z, y = chip // 2, chip % 2
+    other = {"dp": 1 - core}
+
+    def dest(u, c):
+        high = jnp.where(u < 2, 2, jnp.where(u < 6, 3, u - 6))
+        return jnp.where(c == 0, u // 4, high)
+
+    def spot(u, c):
+        high = jnp.where(u < 2, u + 2, jnp.where(u < 6, u - 2, 4))
+        return jnp.where(c == 0, u % 4, high)
+
+    def fetch(s):
+        u = s % count
+        pair = (core == 1) & (u >= 6)
+        parts = (jnp.where(pair, u + 6, 2 * u), jnp.where(pair, u + 10, 2 * u + 1))
+        return [
+            pltpu.make_async_copy(
+                weight_ref.at[:, :, pl.ds(pl.multiple_of(part * HS, HS), HS)],
+                weight.at[s % 2, :, :, pl.ds(i * HS, HS)],
+                w_sem.at[s % 2, i],
+            )
+            for i, part in enumerate(parts)
+        ]
+
+    for copy in fetch(0):
+        copy.start()
+    greet(z, y, core)
+
+    def product(u, stage):
+        s = stage * count + u
+        for copy in fetch(s):
+            copy.wait()
+
+        @pl.when(s + 1 < 2 * count)
+        def _():
+            for copy in fetch(s + 1):
+                copy.start()
+
+        row = y if stage else 1 - y
+        part = pl.ds(pl.multiple_of(row * rows, rows), rows)
+        total = matmul(taps_ref[0, part], weight[s % 2, 0])
+        total += matmul(taps_ref[1, part], weight[s % 2, 1])
+        return total + matmul(taps_ref[2, part], weight[s % 2, 2])
+
+    def out_copy(u, c):
+        place = merged_ref.at[spot(u, c)]
+        return pltpu.make_async_remote_copy(
+            place, place, out_send.at[u], out_recv.at[u], device_id=other, device_id_type=MESH
+        )
+
+    def finish(u, total):
+        merged_ref[spot(u, core)] = total.astype(BF)
+        out_copy(u, core).start()
+
+    sems = (y_send, y_recv, z_send, z_recv)
+    reduce_units(
+        count, z, y, lambda u: dest(u, core), product, finish, yout, own, yin, zin, sems
+    )
+
+    def close(u, _):
+        @pl.when(dest(u, core) == z)
+        def _():
+            out_copy(u, core).wait_send()
+
+        @pl.when(dest(u, 1 - core) == z)
+        def _():
+            out_copy(u, 1 - core).wait_recv()
+
+        return 0
+
+    lax.fori_loop(0, count, close, 0)
+
+
+def units(count, rows):
+    shape = (rows, TILE)
+    return [
+        pltpu.VMEM((count, *shape), BF),
+        pltpu.VMEM((count, *shape), BF),
+        pltpu.VMEM((count, *shape), BF),
+        pltpu.VMEM((2, count, *shape), BF),
+    ]
+
+
+def dma(*shape):
+    return pltpu.SemaphoreType.DMA(shape)
+
+
+def unit_sems(count):
+    return [dma(count), dma(count), dma(count), dma(2, count)]
+
+
+def down_and_sum(hidden_act, down_weight, residual, tap_early, tap_middle):
+    rows, units_in = hidden_act.shape
+    width = residual.shape[1]
+    count = 4 * width // TILE
+    return pl.pallas_call(
+        down_kernel,
+        out_shape=jax.ShapeDtypeStruct((3, 2 * rows, width), BF),
+        in_specs=[pl.BlockSpec(memory_space=pl.ANY)] * 5,
+        out_specs=pl.BlockSpec(memory_space=pltpu.VMEM),
+        scratch_shapes=[
+            pltpu.VMEM((2, rows, units_in), BF),
+            pltpu.VMEM((2, units_in, TILE), BF),
+            pltpu.VMEM((2, rows, width), BF),
+            *units(count, rows),
+            dma(2), dma(4), dma(4), dma(4),
+            *unit_sems(count),
+            dma(count // 2), dma(count // 2),
+        ],
+        compiler_params=pltpu.CompilerParams(
+            collective_id=0, has_side_effects=True, vmem_limit_bytes=56 << 20
+        ),
+        cost_estimate=pl.CostEstimate(
+            flops=4 * rows * units_in * down_weight.shape[1],
+            bytes_accessed=4 * down_weight.size,
+            transcendentals=0,
+        ),
+        name="down_and_sum",
+    )(hidden_act, down_weight, residual, tap_early, tap_middle)
+
+
+def join_and_sum(taps, merge_weight):
+    rows = taps.shape[1] // 2
+    parts, depth, wide = merge_weight.shape
+    count = wide // TILE
+    return pl.pallas_call(
+        join_kernel,
+        out_shape=jax.ShapeDtypeStruct((5, rows, TILE), BF),
+        in_specs=[pl.BlockSpec(memory_space=pltpu.VMEM), pl.BlockSpec(memory_space=pl.ANY)],
+        out_specs=pl.BlockSpec(memory_space=pltpu.VMEM),
+        scratch_shapes=[
+            pltpu.VMEM((2, parts, depth, TILE), BF),
+            *units(count, rows),
+            dma(2, 2),
+            *unit_sems(count),
+            dma(count), dma(count),
+        ],
+        compiler_params=pltpu.CompilerParams(
+            collective_id=1, has_side_effects=True, vmem_limit_bytes=56 << 20
+        ),
+        cost_estimate=pl.CostEstimate(
+            flops=4 * rows * parts * depth * wide,
+            bytes_accessed=4 * merge_weight.size,
+            transcendentals=0,
+        ),
+        name="join_and_sum",
+    )(taps, merge_weight)
+
+
+def plain_sums(hidden_act, down_weight, residual, tap_early, tap_middle, merge_weight):
+    rows = hidden_act.shape[0]
+    chips = lax.axis_size("tensor")
+    core = lax.axis_index("dp")
+    per_core = QH // chips
+    wide = (per_core + 1) * HS
+    hidden = lax.all_gather(hidden_act, "dp", axis=0, tiled=True)
+    taps = lax.all_gather(jnp.concatenate([tap_early, tap_middle], axis=1), "dp", axis=0, tiled=True)
+    partial_sum = jnp.dot(hidden, down_weight, preferred_element_type=F32).astype(BF)
+    partial_sum = lax.all_to_all(partial_sum, "dp", split_axis=0, concat_axis=1, tiled=True)
+    summed = lax.psum_scatter(partial_sum, "tensor", scatter_dimension=1, tiled=True).astype(F32)
+    tap_late = (residual.astype(F32) + summed).astype(BF)
+    late = lax.all_gather(tap_late, "dp", axis=0, tiled=True)
+
+    weight = own_columns(merge_weight, core, per_core)
+    joined = jnp.dot(taps, weight[:2].reshape(-1, weight.shape[2]), preferred_element_type=F32)
+    joined = (joined + jnp.dot(late, weight[2], preferred_element_type=F32)).astype(BF)
+    joined = joined.reshape(2, rows, chips // 2, wide).transpose(2, 0, 1, 3)
+    merged = lax.psum_scatter(
+        joined.reshape(chips, rows, wide), "tensor", scatter_dimension=0, tiled=False
+    )
+    query, mine_kv = merged[:, : per_core * HS], merged[:, per_core * HS :]
+    other_kv = swap(mine_kv)
+    key = jnp.where(core == 0, mine_kv, other_kv)
+    value = jnp.where(core == 0, other_kv, mine_kv)
+    return query, key, value
+
+
+def chain_sums(hidden_act, down_weight, residual, tap_early, tap_middle, merge_weight):
+    taps = down_and_sum(hidden_act, down_weight, residual, tap_early, tap_middle)
+    merged = join_and_sum(taps, merge_weight)
+    query = jnp.where(lax.axis_index("dp") == 0, merged[:2], merged[2:4])
+    query = jnp.concatenate([query[0], query[1]], axis=1)
+    return query, merged[4, :, :HS], merged[4, :, HS:]
 
 
 def local(
@@ -85,27 +507,12 @@
     core = lax.axis_index("dp")
     chip = lax.axis_index("tensor")
     per_core = QH // chips
-    wide = (per_core + 1) * HS
     n_seq = lengths.shape[1]
 
-    hidden = lax.all_gather(hidden_act, "dp", axis=0, tiled=True)
     table = jnp.concatenate([lengths[0], offsets[0], owner_map[0], loss_mask])
     tables = lax.all_gather(table, "dp", axis=0, tiled=False)
-    taps = lax.all_gather(jnp.concatenate([tap_early, tap_middle], axis=1), "dp", axis=0, tiled=True)
-
-    partial_sum = jnp.dot(hidden, down_weight, preferred_element_type=F32).astype(BF)
-    partial_sum = lax.all_to_all(partial_sum, "dp", split_axis=0, concat_axis=1, tiled=True)
-    summed = lax.psum_scatter(partial_sum, "tensor", scatter_dimension=1, tiled=True).astype(F32)
-    tap_late = (residual.astype(F32) + summed).astype(BF)
-    late = lax.all_gather(tap_late, "dp", axis=0, tiled=True)
-
-    weight = own_columns(merge_weight, core, per_core)
-    joined = jnp.dot(taps, weight[:2].reshape(-1, weight.shape[2]), preferred_element_type=F32)
-    joined = (joined + jnp.dot(late, weight[2], preferred_element_type=F32)).astype(BF)
-    joined = joined.reshape(2, rows, chips // 2, wide).transpose(2, 0, 1, 3)
-    merged = lax.psum_scatter(
-        joined.reshape(chips, rows, wide), "tensor", scatter_dimension=0, tiled=False
-    )
+    sums = chain_sums if chips == 8 else plain_sums
+    query, key, value = sums(hidden_act, down_weight, residual, tap_early, tap_middle, merge_weight)
 
     row = chip % 2
     mine = jnp.where(row == 0, tables[0], tables[1])
@@ -121,10 +528,6 @@
     slot = token + jnp.sum(jnp.where(inside, start[None, :], 0), axis=1)
     place = (jnp.arange(chips * capacity, dtype=jnp.int32)[:, None] == slot[None, :]).astype(BF)
 
-    query, mine_kv = merged[:, : per_core * HS], merged[:, per_core * HS :]
-    other_kv = swap(mine_kv)
-    key = jnp.where(core == 0, mine_kv, other_kv)
-    value = jnp.where(core == 0, other_kv, mine_kv)
     result = attend(query, key, value, sequence, keep, q_gain, k_gain)
     slots = jnp.dot(place, result, preferred_element_type=F32).astype(BF)
     slots = lax.all_to_all(

time: 421 us -> 210 us (0.50)
  the two profiles are of different devices: /device:TPU:14 before, /device:TPU:0 now
where the time goes in v2:
time: 210 us; the launch traced here: 208 us
  Pallas kernels  156 us (74%)
  blocking collectives  37.6 us (18%)
  other arithmetic  4.3 us (2%)
  matrix products  3.93 us (2%)
  local copies, waits for them, and re-layouts  3.86 us (2%)
    pallas_call x1, Pallas kernels, down_and_sum(): pl.pallas_call(down_kernel, out_shape=jax.ShapeDtypeStruct((3, 2 * rows,...  100 us
    pallas_call x1, Pallas kernels, join_and_sum(): pl.pallas_call(join_kernel, out_shape=jax.ShapeDtypeStruct((5, rows, TILE...  55.9 us
    all_to_all x1, blocking collectives, local(): lax.all_to_all(slots.reshape(chips, capacity, per_core * HS), 'tensor', s...  35.7 us
  transfers between devices with their start and end apart: 1, of which 1 were waited for; matrix products, arithmetic and copies ran while one was open for 0% of the time, Pallas kernels for 0%

profile of v2, /device:TPU:0, one launch (start us, length us, event | category | flops | bytes accessed | tf_op | source)
XLA Modules:
  0.0 208.3 jit_solution(13834618859557589350)
XLA Ops:
  0.0 1.2 dynamic-slice
  1.9 0.9 add_dynamic-update-slice_fusion
  2.8 1.9 all-reduce
  4.7 0.1 slice_select_fusion.1
  4.8 0.1 slice_bitcast_fusion.4
  4.9 0.1 fusion.47
  5.0 0.2 select_reduce_fusion.2
  5.1 0.1 fusion.53
  5.2 0.1 select_reduce_fusion.1
  5.3 0.1 fusion.11
  5.5 100.0 %down_and_sum.1.taps_ref = bf16[3,768,1024]{2,1,0:T(8,128)(2,1)} custom-call(bf16[384,3584]{1,0:T(8,128)(2,1)} %hidden_ref.1, bf16[3584,4096]{1,0:T(8,128)(2,1)} %weight_ref.2, bf16[384,1024]{1,0:T(8,128)(2,1)} %residual_ref.1, bf16[384,1024]{1,0:T(8,128)(2,1)} %early_ref.1, bf16[384,1024]{1,0:T(8,128)(2,1)} %middle_ref.1), custom_call_target="tpu_custom_call" | custom-call | flops 22548578304 | bytes 58720256 | tf_op jit(solution)/shard_map/down_and_sum/pallas_call | solution.py:400
  105.5 55.9 %join_and_sum.1 = bf16[5,384,256]{2,1,0:T(8,128)(2,1)} custom-call(bf16[3,768,1024]{2,1,0:T(8,128)(2,1)} %down_and_sum.1.taps_ref, bf16[3,1024,2560]{2,1,0:T(8,128)(2,1)} %weight_ref.3), custom_call_target="tpu_custom_call" | custom-call | flops 12079595520 | bytes 31457280 | tf_op jit(solution)/shard_map/join_and_sum/pallas_call | solution.py:430
  161.4 0.0 copy-start
  161.4 0.0 copy-start.1
  161.4 1.0 fusion.21
  162.5 1.2 slice_select_fusion
  163.7 0.1 concatenate.12
  163.8 0.1 concatenate.13
  163.9 0.3 fusion.6
  164.2 0.0 copy-done
  164.2 0.0 copy-done.1
  164.2 2.0 fusion.55
  166.2 1.3 fusion.4
  167.5 0.1 fusion.10
  167.6 0.6 convolution_convert_fusion
  168.2 0.2 reshape.69
  168.4 35.7 %all_to_all.5 = bf16[8,94,512]{2,1,0:T(8,128)(2,1)S(1)} all-to-all(bf16[8,94,512]{2,1,0:T(8,128)(2,1)S(1)} %reshape.69), channel_id=1, replica_groups=mesh['groups'=2,'tensor'=8,'dp'=2] {'tensor'}, dimensions={0} | all-to-all | bytes 1540096 | tf_op jit(solution)/shard_map/all_to_all | solution.py:533
  204.2 0.1 collective-permute-start
  204.3 1.7 collective-permute-done
  206.0 0.1 fusion.13
  206.0 0.1 maximum_bitcast_fusion
  206.1 0.8 copy.39
  206.9 1.3 reshape.71
  (8 shorter events, 0.1 us)
Async XLA Ops:
  161.4 2.8 %copy-start = (f32[128]{0:T(128)S(1)}, f32[128]{0:T(128)}, u32[]{:S(2)}) copy-start(f32[128]{0:T(128)} %param.18) | copy-start | bytes 1540
  161.4 2.8 %copy-start.1 = (f32[128]{0:T(128)S(1)}, f32[128]{0:T(128)}, u32[]{:S(2)}) copy-start(f32[128]{0:T(128)} %param.19) | copy-start | bytes 1540
  204.2 1.8 collective-permute-start

commit v3 on v2

--- a/solution.py
+++ b/solution.py
@@ -75,20 +75,18 @@
     return jnp.dot(a, b, preferred_element_type=F32)
 
 
-def greet(z, y, core):
+def greet(me):
     barrier = pltpu.get_barrier_semaphore()
-    pl.semaphore_signal(barrier, 1, device_id={"tensor": z * 2 + 1 - y}, device_id_type=MESH)
-    pl.semaphore_signal(barrier, 1, device_id={"dp": 1 - core}, device_id_type=MESH)
-
-    @pl.when(z > 0)
-    def _():
-        pl.semaphore_signal(barrier, 1, device_id={"tensor": (z - 1) * 2 + y}, device_id_type=MESH)
-
-    @pl.when(z < 3)
-    def _():
-        pl.semaphore_signal(barrier, 1, device_id={"tensor": (z + 1) * 2 + y}, device_id_type=MESH)
-
-    pl.semaphore_wait(barrier, jnp.where((z == 0) | (z == 3), 3, 4))
+
+    def signal(i, _):
+        peer = (me + i) % 16
+        pl.semaphore_signal(
+            barrier, 1, device_id={"tensor": peer // 2, "dp": peer % 2}, device_id_type=MESH
+        )
+        return 0
+
+    lax.fori_loop(1, 16, signal, 0)
+    pl.semaphore_wait(barrier, 15)
 
 
 def reduce_units(count, z, y, dest, product, finish, yout, own, yin, zin, sems):
@@ -185,11 +183,11 @@
     lax.fori_loop(0, count, last, 0)
 
 
-def down_kernel(
-    hidden_ref, weight_ref, residual_ref, early_ref, middle_ref, taps_ref,
-    hidden, weight, res, yout, own, yin, zin,
-    w_sem, in_sem, far_send, far_recv, y_send, y_recv, z_send, z_recv, out_send, out_recv,
+def down_part(
+    ins, taps_ref, hidden, weight, res, tab, yout, own, yin, zin,
+    w_sem, in_sem, far_send, far_recv, y_send, y_recv, z_send, z_recv, out_send, out_recv, warm_up,
 ):
+    hidden_ref, weight_ref, residual_ref, early_ref, middle_ref = ins
     rows, width = residual_ref.shape
     tiles = width // TILE
     count = 4 * tiles
@@ -213,12 +211,14 @@
     ]
     near[0].start()
     fetch(0).start()
-    greet(z, y, core)
+    warm_up()
+    greet(chip * 2 + core)
     pairs = [
         (hidden_ref, hidden.at[1]),
         (residual_ref, res.at[1]),
         (early_ref, taps_ref.at[0, mine]),
         (middle_ref, taps_ref.at[1, mine]),
+        (tab.at[0], tab.at[1]),
     ]
     far = [
         pltpu.make_async_remote_copy(
@@ -294,9 +294,22 @@
         copy.wait_recv()
 
 
-def join_kernel(
-    taps_ref, weight_ref, merged_ref,
-    weight, yout, own, yin, zin,
+def join_fetch(s, count, core, weight_ref, weight, w_sem):
+    u = s % count
+    pair = (core == 1) & (u >= 6)
+    parts = (jnp.where(pair, u + 6, 2 * u), jnp.where(pair, u + 10, 2 * u + 1))
+    return [
+        pltpu.make_async_copy(
+            weight_ref.at[:, :, pl.ds(pl.multiple_of(part * HS, HS), HS)],
+            weight.at[s % 2, :, :, pl.ds(i * HS, HS)],
+            w_sem.at[s % 2, i],
+        )
+        for i, part in enumerate(parts)
+    ]
+
+
+def join_part(
+    taps_ref, weight_ref, merged_ref, weight, yout, own, yin, zin,
     w_sem, y_send, y_recv, z_send, z_recv, out_send, out_recv,
 ):
     rows = merged_ref.shape[1]
@@ -314,21 +327,7 @@
         return jnp.where(c == 0, u % 4, high)
 
     def fetch(s):
-        u = s % count
-        pair = (core == 1) & (u >= 6)
-        parts = (jnp.where(pair, u + 6, 2 * u), jnp.where(pair, u + 10, 2 * u + 1))
-        return [
-            pltpu.make_async_copy(
-                weight_ref.at[:, :, pl.ds(pl.multiple_of(part * HS, HS), HS)],
-                weight.at[s % 2, :, :, pl.ds(i * HS, HS)],
-                w_sem.at[s % 2, i],
-            )
-            for i, part in enumerate(parts)
-        ]
-
-    for copy in fetch(0):
-        copy.start()
-    greet(z, y, core)
+        return join_fetch(s, count, core, weight_ref, weight, w_sem)
 
     def product(u, stage):
         s = stage * count + u
@@ -373,6 +372,138 @@
         return 0
 
     lax.fori_loop(0, count, close, 0)
+
+
+def attend_part(
+    merged_ref, tab, q_gain_ref, k_gain_ref, out_ref, result, slots, slot_send, slot_recv, n_seq, capacity
+):
+    rows = merged_ref.shape[1]
+    chip, core = lax.axis_index("tensor"), lax.axis_index("dp")
+    z, y = chip // 2, chip % 2
+    table = tab[(core + y) % 2]
+    length, offset, owner = [table[i : i + 1, :n_seq] for i in range(3)]
+    keep = table[3:4]
+    across = lax.broadcasted_iota(jnp.int32, (n_seq, n_seq), 1)
+    down = lax.broadcasted_iota(jnp.int32, (n_seq, n_seq), 0)
+
+    def upright(x):
+        return jnp.sum(jnp.where(across == down, x, 0), axis=1, keepdims=True)
+
+    length_up, offset_up, owner_up = upright(length), upright(offset), upright(owner)
+    earlier = (owner == owner_up) & (across < down)
+    base_up = jnp.sum(jnp.where(earlier, length, 0), axis=1, keepdims=True)
+    start_up = owner_up * capacity + base_up - offset_up
+    token = lax.broadcasted_iota(jnp.int32, (n_seq, rows), 1)
+    inside = (offset_up <= token) & (token < offset_up + length_up)
+    index = lax.broadcasted_iota(jnp.int32, (n_seq, rows), 0)
+    sequence = jnp.sum(jnp.where(inside, index, 0), axis=0, keepdims=True)
+    slot = jnp.sum(jnp.where(inside, start_up + token, 0), axis=0, keepdims=True)
+    slot = jnp.where(keep == 1, slot, -1)
+    token_up = lax.broadcasted_iota(jnp.int32, (rows, n_seq), 0)
+    inside_up = (offset <= token_up) & (token_up < offset + length)
+    index_up = lax.broadcasted_iota(jnp.int32, (rows, n_seq), 1)
+    sequence_up = jnp.sum(jnp.where(inside_up, index_up, 0), axis=1, keepdims=True)
+    later = lax.broadcasted_iota(jnp.int32, (rows, rows), 0)
+    place = lax.broadcasted_iota(jnp.int32, (rows, rows), 1)
+    allowed = (sequence_up == sequence) & (place <= later)
+
+    key = norm(merged_ref[4, :, :HS].astype(F32), k_gain_ref[...]).astype(BF)
+    value = merged_ref[4, :, HS:]
+    for head in range(4):
+        lanes = slice(head % 2 * HS, head % 2 * HS + HS)
+        query = merged_ref[2 * core + head // 2, :, lanes].astype(F32)
+        query = norm(query, q_gain_ref[...]).astype(BF)
+        scores = lax.dot_general(
+            query, key, (((1,), (1,)), ((), ())), preferred_element_type=F32
+        ) / math.sqrt(HS)
+        scores = jnp.where(allowed, scores, -1e30)
+        expo = jnp.exp(scores - jnp.max(scores, axis=-1, keepdims=True))
+        weights = (expo / jnp.sum(expo, axis=-1, keepdims=True)).astype(BF)
+        result[:, head * HS : (head + 1) * HS] = matmul(weights, value).astype(BF)
+
+    padded, wide = slots.shape[1:]
+
+    def slot_copy(o, source):
+        columns = pl.ds(pl.multiple_of(source * wide, wide), wide)
+        return pltpu.make_async_remote_copy(
+            slots.at[o], out_ref.at[:, columns], slot_send.at[o], slot_recv.at[source],
+            device_id={"tensor": o, "dp": y}, device_id_type=MESH,
+        )
+
+    source = 2 * z + core
+    which = lax.broadcasted_iota(jnp.int32, (padded, rows), 0)
+
+    def send(i, _):
+        o = (chip + 1 + i) % 8
+        hit = (which + o * capacity == slot) & (which < capacity)
+        slots[o] = matmul(jnp.where(hit, 1.0, 0.0).astype(BF), result[...]).astype(BF)
+        local = (o == chip) & (core == y)
+
+        @pl.when(local)
+        def _():
+            out_ref[:, pl.ds(pl.multiple_of(source * wide, wide), wide)] = slots[o]
+
+        @pl.when(jnp.logical_not(local))
+        def _():
+            slot_copy(o, source).start()
+
+        return 0
+
+    lax.fori_loop(0, 8, send, 0)
+
+    def close(i, _):
+        @pl.when(jnp.logical_not((i == chip) & (core == y)))
+        def _():
+            slot_copy(i, source).wait_send()
+
+        @pl.when(jnp.logical_not((i == source) & (core == y)))
+        def _():
+            slot_copy(chip, i).wait_recv()
+
+        return 0
+
+    lax.fori_loop(0, 8, close, 0)
+
+
+def whole_kernel(
+    hidden_ref, down_ref, residual_ref, early_ref, middle_ref, merge_ref,
+    q_gain_ref, k_gain_ref, length_ref, offset_ref, owner_ref, mask_ref,
+    out_ref,
+    taps, merged, tab, result, slots,
+    hidden, weight, res, yout, own, yin, zin,
+    w_sem, in_sem, far_send, far_recv, y_send, y_recv, z_send, z_recv, out_send, out_recv,
+    weight2, yout2, own2, yin2, zin2,
+    w_sem2, y_send2, y_recv2, z_send2, z_recv2, out_send2, out_recv2,
+    slot_send, slot_recv,
+):
+    n_seq = length_ref.shape[1]
+    capacity = residual_ref.shape[0] // 4 - 2
+
+    def warm_up():
+        copies = join_fetch(
+            0, merge_ref.shape[2] // TILE, lax.axis_index("dp"), merge_ref, weight2, w_sem2
+        )
+        for copy in copies:
+            copy.start()
+        tab[0] = jnp.zeros(tab.shape[1:], jnp.int32)
+        tab[0, 0:1, :n_seq] = length_ref[...]
+        tab[0, 1:2, :n_seq] = offset_ref[...]
+        tab[0, 2:3, :n_seq] = owner_ref[...]
+        tab[0, 3:4] = mask_ref[...]
+
+    down_part(
+        (hidden_ref, down_ref, residual_ref, early_ref, middle_ref), taps,
+        hidden, weight, res, tab, yout, own, yin, zin,
+        w_sem, in_sem, far_send, far_recv, y_send, y_recv, z_send, z_recv, out_send, out_recv, warm_up,
+    )
+    join_part(
+        taps, merge_ref, merged, weight2, yout2, own2, yin2, zin2,
+        w_sem2, y_send2, y_recv2, z_send2, z_recv2, out_send2, out_recv2,
+    )
+    attend_part(
+        merged, tab, q_gain_ref, k_gain_ref, out_ref, result, slots, slot_send, slot_recv,
+        n_seq, capacity,
+    )
 
 
 def units(count, rows):
@@ -393,62 +524,67 @@
     return [dma(count), dma(count), dma(count), dma(2, count)]
 
 
-def down_and_sum(hidden_act, down_weight, residual, tap_early, tap_middle):
-    rows, units_in = hidden_act.shape
+def grid_local(
+    hidden_act,
+    down_weight,
+    residual,
+    tap_early,
+    tap_middle,
+    merge_weight,
+    q_gain,
+    k_gain,
+    lengths,
+    offsets,
+    owner_map,
+    loss_mask,
+):
+    rows, depth = hidden_act.shape
     width = residual.shape[1]
     count = 4 * width // TILE
-    return pl.pallas_call(
-        down_kernel,
-        out_shape=jax.ShapeDtypeStruct((3, 2 * rows, width), BF),
-        in_specs=[pl.BlockSpec(memory_space=pl.ANY)] * 5,
+    parts, features, wide = merge_weight.shape
+    count2 = wide // TILE
+    capacity = rows // 4 - 2
+    padded = -(-capacity // 16) * 16
+    out = pl.pallas_call(
+        whole_kernel,
+        out_shape=jax.ShapeDtypeStruct((padded, QH * HS), BF),
+        in_specs=[pl.BlockSpec(memory_space=pl.ANY)] * 6 + [pl.BlockSpec(memory_space=pltpu.VMEM)] * 6,
         out_specs=pl.BlockSpec(memory_space=pltpu.VMEM),
         scratch_shapes=[
-            pltpu.VMEM((2, rows, units_in), BF),
-            pltpu.VMEM((2, units_in, TILE), BF),
+            pltpu.VMEM((3, 2 * rows, width), BF),
+            pltpu.VMEM((5, rows, TILE), BF),
+            pltpu.VMEM((2, 8, rows), jnp.int32),
+            pltpu.VMEM((rows, 4 * HS), BF),
+            pltpu.VMEM((8, padded, 4 * HS), BF),
+            pltpu.VMEM((2, rows, depth), BF),
+            pltpu.VMEM((2, depth, TILE), BF),
             pltpu.VMEM((2, rows, width), BF),
             *units(count, rows),
-            dma(2), dma(4), dma(4), dma(4),
+            dma(2), dma(4), dma(5), dma(5),
             *unit_sems(count),
             dma(count // 2), dma(count // 2),
+            pltpu.VMEM((2, parts, features, TILE), BF),
+            *units(count2, rows),
+            dma(2, 2),
+            *unit_sems(count2),
+            dma(count2), dma(count2),
+            dma(8), dma(8),
         ],
         compiler_params=pltpu.CompilerParams(
-            collective_id=0, has_side_effects=True, vmem_limit_bytes=56 << 20
+            collective_id=0, has_side_effects=True, vmem_limit_bytes=60 << 20
         ),
         cost_estimate=pl.CostEstimate(
-            flops=4 * rows * units_in * down_weight.shape[1],
-            bytes_accessed=4 * down_weight.size,
+            flops=4 * rows * (depth * down_weight.shape[1] + parts * features * wide),
+            bytes_accessed=4 * (down_weight.size + merge_weight.size),
             transcendentals=0,
         ),
-        name="down_and_sum",
-    )(hidden_act, down_weight, residual, tap_early, tap_middle)
-
-
-def join_and_sum(taps, merge_weight):
-    rows = taps.shape[1] // 2
-    parts, depth, wide = merge_weight.shape
-    count = wide // TILE
-    return pl.pallas_call(
-        join_kernel,
-        out_shape=jax.ShapeDtypeStruct((5, rows, TILE), BF),
-        in_specs=[pl.BlockSpec(memory_space=pltpu.VMEM), pl.BlockSpec(memory_space=pl.ANY)],
-        out_specs=pl.BlockSpec(memory_space=pltpu.VMEM),
-        scratch_shapes=[
-            pltpu.VMEM((2, parts, depth, TILE), BF),
-            *units(count, rows),
-            dma(2, 2),
-            *unit_sems(count),
-            dma(count), dma(count),
-        ],
-        compiler_params=pltpu.CompilerParams(
-            collective_id=1, has_side_effects=True, vmem_limit_bytes=56 << 20
-        ),
-        cost_estimate=pl.CostEstimate(
-            flops=4 * rows * parts * depth * wide,
-            bytes_accessed=4 * merge_weight.size,
-            transcendentals=0,
-        ),
-        name="join_and_sum",
-    )(taps, merge_weight)
+        name="whole",
+    )(
+        hidden_act, down_weight, residual, tap_early, tap_middle, merge_weight,
+        q_gain.reshape(1, HS), k_gain.reshape(1, HS), lengths, offsets, owner_map,
+        loss_mask.reshape(1, rows),
+    )
+    return out[:capacity]
 
 
 def plain_sums(hidden_act, down_weight, residual, tap_early, tap_middle, merge_weight):
@@ -477,14 +613,6 @@
     key = jnp.where(core == 0, mine_kv, other_kv)
     value = jnp.where(core == 0, other_kv, mine_kv)
     return query, key, value
-
-
-def chain_sums(hidden_act, down_weight, residual, tap_early, tap_middle, merge_weight):
-    taps = down_and_sum(hidden_act, down_weight, residual, tap_early, tap_middle)
-    merged = join_and_sum(taps, merge_weight)
-    query = jnp.where(lax.axis_index("dp") == 0, merged[:2], merged[2:4])
-    query = jnp.concatenate([query[0], query[1]], axis=1)
-    return query, merged[4, :, :HS], merged[4, :, HS:]
 
 
 def local(
@@ -511,8 +639,7 @@
 
     table = jnp.concatenate([lengths[0], offsets[0], owner_map[0], loss_mask])
     tables = lax.all_gather(table, "dp", axis=0, tiled=False)
-    sums = chain_sums if chips == 8 else plain_sums
-    query, key, value = sums(hidden_act, down_weight, residual, tap_early, tap_middle, merge_weight)
+    query, key, value = plain_sums(hidden_act, down_weight, residual, tap_early, tap_middle, merge_weight)
 
     row = chip % 2
     mine = jnp.where(row == 0, tables[0], tables[1])
@@ -544,8 +671,10 @@
 
 
 def solution(mesh):
+    shape = mesh.shape
+    grid = shape["tensor"] == 8 and shape["dp"] == 2
     return jax.shard_map(
-        local,
+        grid_local if grid else local,
         mesh=mesh,
         in_specs=(
             P(("groups", "dp"), "tensor"),

time: 210 us -> 187 us (0.89)
  the two profiles are of different devices: /device:TPU:0 before, /device:TPU:14 now
where the time goes in v3:
time: 187 us; the launch traced here: 185 us
  Pallas kernels  182 us (97%)
  local copies, waits for them, and re-layouts  3.31 us (2%)
    pallas_call x1, Pallas kernels, grid_local(): pl.pallas_call(whole_kernel, out_shape=jax.ShapeDtypeStruct((padded, QH *...  182 us

profile of v3, /device:TPU:14, one launch (start us, length us, event | category | flops | bytes accessed | tf_op | source)
XLA Modules:
  0.0 185.2 jit_solution(17913170289990196086)
XLA Ops:
  0.0 1.2 reshape.11.mask_ref
  1.2 181.9 %whole.1 = bf16[96,4096]{1,0:T(8,128)(2,1)} custom-call(bf16[384,3584]{1,0:T(8,128)(2,1)} %hidden_ref.1, bf16[3584,4096]{1,0:T(8,128)(2,1)} %down_ref.1, bf16[384,1024]{1,0:T(8,128)(2,1)} %residual_ref.1, bf16[384,1024]{1,0:T(8,128)(2,1)} %early_ref.1, bf16[384,1024]{1,0:T(8,128)(2,1)} %middle_ref.1, bf16[3,1024,2560]{2,1,0:T(8,128)(2,1)} %merge_ref.1, ...), custom_call_target="tpu_custom_call" | custom-call | flops 34628173824 | bytes 90177536 | tf_op jit(solution)/shard_map/whole/pallas_call | solution.py:548
  183.1 2.1 %copy.14 = bf16[94,4096]{1,0:T(8,128)(2,1)} copy(bf16[94,4096]{1,0:T(8,128)(2,1)} %bitcast.3) | data formatting | bytes 1540096

commit v4 on v3

--- a/solution.py
+++ b/solution.py
@@ -89,115 +89,127 @@
     pl.semaphore_wait(barrier, 15)
 
 
-def reduce_units(count, z, y, dest, product, finish, yout, own, yin, zin, sems):
-    y_send, y_recv, z_send, z_recv = sems
-
-    def y_copy(u):
+AHEAD = 3
+
+
+class Reduction:
+    def __init__(self, count, z, y, dest, product, finish, buffers, sems):
+        self.count, self.z, self.y, self.dest = count, z, y, dest
+        self.product, self.finish = product, finish
+        self.yout, self.own, self.yin, self.zin = buffers
+        self.y_send, self.y_recv, self.z_send, self.z_recv = sems
+
+    def y_copy(self, u):
         return pltpu.make_async_remote_copy(
-            yout.at[u], yin.at[u], y_send.at[u], y_recv.at[u],
-            device_id={"tensor": z * 2 + 1 - y}, device_id_type=MESH,
+            self.yout.at[u], self.yin.at[u], self.y_send.at[u], self.y_recv.at[u],
+            device_id={"tensor": self.z * 2 + 1 - self.y}, device_id_type=MESH,
         )
 
-    def z_copy(u, way):
-        target = (z + 1 + 2 * way) % 4
+    def z_copy(self, u, way):
+        target = (self.z + 1 + 2 * way) % 4
         return pltpu.make_async_remote_copy(
-            own.at[u], zin.at[way, u], z_send.at[u], z_recv.at[way, u],
-            device_id={"tensor": target * 2 + y}, device_id_type=MESH,
+            self.own.at[u], self.zin.at[way, u], self.z_send.at[u], self.z_recv.at[way, u],
+            device_id={"tensor": target * 2 + self.y}, device_id_type=MESH,
         )
 
-    def first(u, _):
-        yout[u] = product(u, 0).astype(BF)
-        y_copy(u).start()
-        return 0
-
-    lax.fori_loop(0, count, first, 0)
-
-    def pass_on(i, way, place, edge):
-        u = i - place
-
-        @pl.when((u >= 0) & (u < count))
-        def _():
-            ahead = dest(u) - z if way == 0 else z - dest(u)
+    def first(self, u):
+        self.yout[u] = self.product(u, 0).astype(BF)
+
+        @pl.when(u >= AHEAD)
+        def _():
+            self.y_copy(u - AHEAD).wait_send()
+
+        self.y_copy(u).start()
+
+    def second(self, u):
+        self.own[u] = self.product(u, 1).astype(BF)
+
+    def pair(self, u):
+        return self.own[u].astype(F32) + self.yin[u].astype(F32)
+
+    def pass_on(self, u, way, edge):
+        z, own, zin = self.z, self.own, self.zin
+
+        @pl.when((u >= 0) & (u < self.count))
+        def _():
+            ahead = self.dest(u) - z if way == 0 else z - self.dest(u)
 
             @pl.when(ahead > 0)
             def _():
-                y_copy(u).wait_recv()
+                self.y_copy(u).wait_recv()
 
                 @pl.when(z == edge)
                 def _():
-                    own[u] = (own[u].astype(F32) + yin[u].astype(F32)).astype(BF)
+                    own[u] = self.pair(u).astype(BF)
 
                 @pl.when(z != edge)
                 def _():
-                    z_copy(u, way).wait_recv()
-                    total = own[u].astype(F32) + yin[u].astype(F32) + zin[way, u].astype(F32)
-                    own[u] = total.astype(BF)
-
-                z_copy(u, way).start()
-
-    def second(i, _):
-        @pl.when(i < count)
-        def _():
-            own[i] = product(i, 1).astype(BF)
-
-        pass_on(i, 0, z, 0)
-        pass_on(i, 1, 3 - z, 3)
+                    self.z_copy(u, way).wait_recv()
+                    own[u] = (self.pair(u) + zin[way, u].astype(F32)).astype(BF)
+
+                self.z_copy(u, way).start()
+
+    def chains(self, i):
+        z, zin = self.z, self.zin
+        self.pass_on(i - z, 0, 0)
+        self.pass_on(i - 3 + z, 1, 3)
         u = i - 3
 
-        @pl.when(u >= 0)
-        def _():
-            @pl.when(dest(u) == z)
+        @pl.when((u >= 0) & (u < self.count))
+        def _():
+            @pl.when(self.dest(u) == z)
             def _():
-                y_copy(u).wait_recv()
+                self.y_copy(u).wait_recv()
 
                 @pl.when(z == 0)
                 def _():
-                    z_copy(u, 1).wait_recv()
-                    finish(u, own[u].astype(F32) + yin[u].astype(F32) + zin[1, u].astype(F32))
+                    self.z_copy(u, 1).wait_recv()
+                    self.finish(u, self.pair(u) + zin[1, u].astype(F32))
 
                 @pl.when(z == 3)
                 def _():
-                    z_copy(u, 0).wait_recv()
-                    finish(u, own[u].astype(F32) + yin[u].astype(F32) + zin[0, u].astype(F32))
+                    self.z_copy(u, 0).wait_recv()
+                    self.finish(u, self.pair(u) + zin[0, u].astype(F32))
 
                 @pl.when((z > 0) & (z < 3))
                 def _():
-                    z_copy(u, 0).wait_recv()
-                    z_copy(u, 1).wait_recv()
-                    total = own[u].astype(F32) + yin[u].astype(F32)
-                    finish(u, total + zin[0, u].astype(F32) + zin[1, u].astype(F32))
-
-        return 0
-
-    lax.fori_loop(0, count + 3, second, 0)
-
-    def last(u, _):
-        y_copy(u).wait_send()
-
-        @pl.when(dest(u) != z)
-        def _():
-            z_copy(u, 0).wait_send()
-
-        return 0
-
-    lax.fori_loop(0, count, last, 0)
-
-
-def down_part(
-    ins, taps_ref, hidden, weight, res, tab, yout, own, yin, zin,
-    w_sem, in_sem, far_send, far_recv, y_send, y_recv, z_send, z_recv, out_send, out_recv, warm_up,
+                    self.z_copy(u, 0).wait_recv()
+                    self.z_copy(u, 1).wait_recv()
+                    self.finish(u, self.pair(u) + zin[0, u].astype(F32) + zin[1, u].astype(F32))
+
+    def close(self):
+        for u in range(self.count - AHEAD, self.count):
+            self.y_copy(u).wait_send()
+
+        def last(u, _):
+            @pl.when(self.dest(u) != self.z)
+            def _():
+                self.z_copy(u, 0).wait_send()
+
+            return 0
+
+        lax.fori_loop(0, self.count, last, 0)
+
+
+def sums_part(
+    ins, merge_ref, taps_ref, merged_ref, tab, fill_tab,
+    hidden, weight, res, yout, own, yin, zin,
+    w_sem, in_sem, far_send, far_recv, y_send, y_recv, z_send, z_recv, out_send, out_recv,
+    weight2, yout2, own2, yin2, zin2,
+    w_sem2, y_send2, y_recv2, z_send2, z_recv2, out_send2, out_recv2,
 ):
     hidden_ref, weight_ref, residual_ref, early_ref, middle_ref = ins
     rows, width = residual_ref.shape
     tiles = width // TILE
     count = 4 * tiles
+    half_count = count // 2
     chip, core = lax.axis_index("tensor"), lax.axis_index("dp")
     z, y = chip // 2, chip % 2
     other = {"dp": 1 - core}
     mine = pl.ds(pl.multiple_of(core * rows, rows), rows)
 
     def fetch(s):
-        u, stage = s % count, s // count
+        u, stage = s // 2, s % 2
         block = 2 * (u % 2) + (1 - y) * (1 - stage) + y * stage
         column = block * width + (u // 2) % tiles * TILE
         source = weight_ref.at[:, pl.ds(pl.multiple_of(column, TILE), TILE)]
@@ -211,7 +223,7 @@
     ]
     near[0].start()
     fetch(0).start()
-    warm_up()
+    fill_tab()
     greet(chip * 2 + core)
     pairs = [
         (hidden_ref, hidden.at[1]),
@@ -233,10 +245,14 @@
     for copy in far[1:]:
         copy.start()
 
+    def half_of(u, stage):
+        return (y + stage + u // half_count) % 2
+
     def product(u, stage):
-        s = stage * count + u
-
-        @pl.when(s == count // 2)
+        s = 2 * u + stage
+        late_core = core == y if stage else core != y
+
+        @pl.when((u == 0) & late_core)
         def _():
             far[0].wait_recv()
 
@@ -246,132 +262,163 @@
         def _():
             fetch(s + 1).start()
 
-        return matmul(hidden[u // (count // 2)], weight[s % 2])
-
-    def out_copy(u, source_core):
-        half = (source_core + u // (count // 2)) % 2
-        place = taps_ref.at[
+        return matmul(hidden[(half_of(u, stage) + core) % 2], weight[s % 2])
+
+    def late_place(u):
+        return (
             2,
-            pl.ds(pl.multiple_of(half * rows, rows), rows),
+            pl.ds(pl.multiple_of(half_of(u, 1) * rows, rows), rows),
             pl.ds(pl.multiple_of((u // 2) % tiles * TILE, TILE), TILE),
-        ]
+        )
+
+    def late_copy(u):
+        place = taps_ref.at[late_place(u)]
         return pltpu.make_async_remote_copy(
             place, place, out_send.at[u // 2], out_recv.at[u // 2], device_id=other, device_id_type=MESH
         )
 
+    def finish(u, total):
+        column = pl.ds(pl.multiple_of((u // 2) % tiles * TILE, TILE), TILE)
+        late = total + res[(half_of(u, 1) + core) % 2, :, column].astype(F32)
+        taps_ref[late_place(u)] = late.astype(BF)
+        late_copy(u).start()
+
+    def late_arrived(start):
+        @pl.when(z // 2 != core)
+        def _():
+            for r in range(start, start + tiles):
+                late_copy(2 * r).wait_recv()
+
+    down = Reduction(
+        count, z, y, lambda u: 2 * core + u % 2, product, finish,
+        (yout, own, yin, zin), (y_send, y_recv, z_send, z_recv),
+    )
+
+    count2 = merge_ref.shape[2] // TILE
+    early = 3 + AHEAD
+
+    def dest2(u, c):
+        high = jnp.where(u < 2, 2, jnp.where(u < 6, 3, u - 6))
+        return jnp.where(c == 0, u // 4, high)
+
+    def spot(u, c):
+        high = jnp.where(u < 2, u + 2, jnp.where(u < 6, u - 2, 4))
+        return jnp.where(c == 0, u % 4, high)
+
+    both = 2 * (count2 - early)
+
+    def turn(u, stage):
+        if stage:
+            return jnp.where(u < count2 - early, early + 2 * u + 1, count2 + u)
+        return jnp.where(u < early, u, early + 2 * (u - early))
+
+    def fetch2(n):
+        m = n - early
+        turns = jnp.where(m % 2 == 0, early + m // 2, m // 2)
+        u = jnp.where(m < 0, n, jnp.where(m < both, turns, n - count2))
+        pair = (core == 1) & (u >= 6)
+        parts = (jnp.where(pair, u + 6, 2 * u), jnp.where(pair, u + 10, 2 * u + 1))
+        return [
+            pltpu.make_async_copy(
+                merge_ref.at[:, :, pl.ds(pl.multiple_of(part * HS, HS), HS)],
+                weight2.at[n % 2, :, :, pl.ds(i * HS, HS)],
+                w_sem2.at[n % 2, i],
+            )
+            for i, part in enumerate(parts)
+        ]
+
+    def product2(u, stage):
+        n = turn(u, stage)
+        for copy in fetch2(n):
+            copy.wait()
+
+        @pl.when(n + 1 < 2 * count2)
+        def _():
+            for copy in fetch2(n + 1):
+                copy.start()
+
+        row = y if stage else 1 - y
+        part = pl.ds(pl.multiple_of(row * rows, rows), rows)
+        total = matmul(taps_ref[0, part], weight2[n % 2, 0])
+        total += matmul(taps_ref[1, part], weight2[n % 2, 1])
+        return total + matmul(taps_ref[2, part], weight2[n % 2, 2])
+
+    def merged_copy(u, c):
+        place = merged_ref.at[spot(u, c)]
+        return pltpu.make_async_remote_copy(
+            place, place, out_send2.at[u], out_recv2.at[u], device_id=other, device_id_type=MESH
+        )
+
+    def finish2(u, total):
+        merged_ref[spot(u, core)] = total.astype(BF)
+        merged_copy(u, core).start()
+
+    join = Reduction(
+        count2, z, y, lambda u: dest2(u, core), product2, finish2,
+        (yout2, own2, yin2, zin2), (y_send2, y_recv2, z_send2, z_recv2),
+    )
+
     near[1].wait()
     far[1].wait_recv()
-
-    def finish(u, total):
-        half = (core + u // (count // 2)) % 2
-        column = pl.ds(pl.multiple_of((u // 2) % tiles * TILE, TILE), TILE)
-        late = total + res[u // (count // 2), :, column].astype(F32)
-        taps_ref[2, pl.ds(pl.multiple_of(half * rows, rows), rows), column] = late.astype(BF)
-        out_copy(u, core).start()
-
-    sems = (y_send, y_recv, z_send, z_recv)
-    reduce_units(
-        count, z, y, lambda u: 2 * core + u % 2, product, finish, yout, own, yin, zin, sems
-    )
-
-    def close(r, _):
-        @pl.when(z // 2 == core)
-        def _():
-            out_copy(2 * r, core).wait_send()
-
-        @pl.when(z // 2 != core)
-        def _():
-            out_copy(2 * r, 1 - core).wait_recv()
-
+    for copy in fetch2(0):
+        copy.start()
+
+    def down_step(i, _):
+        down.first(i)
+        down.second(i)
+        down.chains(i - AHEAD)
         return 0
 
-    lax.fori_loop(0, count // 2, close, 0)
+    lax.fori_loop(0, count, down_step, 0)
     for copy in near[2:]:
         copy.wait()
     for copy in far:
         copy.wait_send()
     for copy in far[2:]:
         copy.wait_recv()
-
-
-def join_fetch(s, count, core, weight_ref, weight, w_sem):
-    u = s % count
-    pair = (core == 1) & (u >= 6)
-    parts = (jnp.where(pair, u + 6, 2 * u), jnp.where(pair, u + 10, 2 * u + 1))
-    return [
-        pltpu.make_async_copy(
-            weight_ref.at[:, :, pl.ds(pl.multiple_of(part * HS, HS), HS)],
-            weight.at[s % 2, :, :, pl.ds(i * HS, HS)],
-            w_sem.at[s % 2, i],
-        )
-        for i, part in enumerate(parts)
-    ]
-
-
-def join_part(
-    taps_ref, weight_ref, merged_ref, weight, yout, own, yin, zin,
-    w_sem, y_send, y_recv, z_send, z_recv, out_send, out_recv,
-):
-    rows = merged_ref.shape[1]
-    count = weight_ref.shape[2] // TILE
-    chip, core = lax.axis_index("tensor"), lax.axis_index("dp")
-    z, y = chip // 2, chip % 2
-    other = {"dp": 1 - core}
-
-    def dest(u, c):
-        high = jnp.where(u < 2, 2, jnp.where(u < 6, 3, u - 6))
-        return jnp.where(c == 0, u // 4, high)
-
-    def spot(u, c):
-        high = jnp.where(u < 2, u + 2, jnp.where(u < 6, u - 2, 4))
-        return jnp.where(c == 0, u % 4, high)
-
-    def fetch(s):
-        return join_fetch(s, count, core, weight_ref, weight, w_sem)
-
-    def product(u, stage):
-        s = stage * count + u
-        for copy in fetch(s):
-            copy.wait()
-
-        @pl.when(s + 1 < 2 * count)
-        def _():
-            for copy in fetch(s + 1):
-                copy.start()
-
-        row = y if stage else 1 - y
-        part = pl.ds(pl.multiple_of(row * rows, rows), rows)
-        total = matmul(taps_ref[0, part], weight[s % 2, 0])
-        total += matmul(taps_ref[1, part], weight[s % 2, 1])
-        return total + matmul(taps_ref[2, part], weight[s % 2, 2])
-
-    def out_copy(u, c):
-        place = merged_ref.at[spot(u, c)]
-        return pltpu.make_async_remote_copy(
-            place, place, out_send.at[u], out_recv.at[u], device_id=other, device_id_type=MESH
-        )
-
-    def finish(u, total):
-        merged_ref[spot(u, core)] = total.astype(BF)
-        out_copy(u, core).start()
-
-    sems = (y_send, y_recv, z_send, z_recv)
-    reduce_units(
-        count, z, y, lambda u: dest(u, core), product, finish, yout, own, yin, zin, sems
-    )
+    late_arrived(0)
+
+    def end_step(i, _):
+        join.first(i)
+        down.chains(count + i - AHEAD)
+        return 0
+
+    lax.fori_loop(0, early, end_step, 0)
+    down.close()
+    late_arrived(tiles)
+
+    @pl.when(z // 2 == core)
+    def _():
+        for r in range(2 * tiles):
+            late_copy(2 * r).wait_send()
+
+    def join_step(j, _):
+        @pl.when(j + early < count2)
+        def _():
+            join.first(j + early)
+
+        @pl.when(j < count2)
+        def _():
+            join.second(j)
+
+        join.chains(j)
+        return 0
+
+    lax.fori_loop(0, count2 + 3, join_step, 0)
+    join.close()
 
     def close(u, _):
-        @pl.when(dest(u, core) == z)
-        def _():
-            out_copy(u, core).wait_send()
-
-        @pl.when(dest(u, 1 - core) == z)
-        def _():
-            out_copy(u, 1 - core).wait_recv()
+        @pl.when(dest2(u, core) == z)
+        def _():
+            merged_copy(u, core).wait_send()
+
+        @pl.when(dest2(u, 1 - core) == z)
+        def _():
+            merged_copy(u, 1 - core).wait_recv()
 
         return 0
 
-    lax.fori_loop(0, count, close, 0)
+    lax.fori_loop(0, count2, close, 0)
 
 
 def attend_part(
@@ -479,25 +526,18 @@
     n_seq = length_ref.shape[1]
     capacity = residual_ref.shape[0] // 4 - 2
 
-    def warm_up():
-        copies = join_fetch(
-            0, merge_ref.shape[2] // TILE, lax.axis_index("dp"), merge_ref, weight2, w_sem2
-        )
-        for copy in copies:
-            copy.start()
+    def fill_tab():
         tab[0] = jnp.zeros(tab.shape[1:], jnp.int32)
         tab[0, 0:1, :n_seq] = length_ref[...]
         tab[0, 1:2, :n_seq] = offset_ref[...]
         tab[0, 2:3, :n_seq] = owner_ref[...]
         tab[0, 3:4] = mask_ref[...]
 
-    down_part(
-        (hidden_ref, down_ref, residual_ref, early_ref, middle_ref), taps,
-        hidden, weight, res, tab, yout, own, yin, zin,
-        w_sem, in_sem, far_send, far_recv, y_send, y_recv, z_send, z_recv, out_send, out_recv, warm_up,
-    )
-    join_part(
-        taps, merge_ref, merged, weight2, yout2, own2, yin2, zin2,
+    sums_part(
+        (hidden_ref, down_ref, residual_ref, early_ref, middle_ref), merge_ref, taps, merged, tab, fill_tab,
+        hidden, weight, res, yout, own, yin, zin,
+        w_sem, in_sem, far_send, far_recv, y_send, y_recv, z_send, z_recv, out_send, out_recv,
+        weight2, yout2, own2, yin2, zin2,
         w_sem2, y_send2, y_recv2, z_send2, z_recv2, out_send2, out_recv2,
     )
     attend_part(

time: 187 us -> 172 us (0.920)
  Pallas kernels: 182 us -> 168 us
    pallas_call x1, Pallas kernels: 182 us -> 168 us  [grid_local(): pl.pallas_call(whole_kernel, out_shape=jax.ShapeDtypeStruct((padded, QH *...]
where the time goes in v4:
time: 172 us; the launch traced here: 171 us
  Pallas kernels  168 us (98%)
  local copies, waits for them, and re-layouts  3.31 us (2%)
    pallas_call x1, Pallas kernels, grid_local(): pl.pallas_call(whole_kernel, out_shape=jax.ShapeDtypeStruct((padded, QH *...  168 us

profile of v4, /device:TPU:14, one launch (start us, length us, event | category | flops | bytes accessed | tf_op | source)
XLA Modules:
  0.0 171.4 jit_solution(3223840775837608962)
XLA Ops:
  0.0 1.2 reshape.11.mask_ref
  1.2 168.0 %whole.1 = bf16[96,4096]{1,0:T(8,128)(2,1)} custom-call(bf16[384,3584]{1,0:T(8,128)(2,1)} %hidden_ref.1, bf16[3584,4096]{1,0:T(8,128)(2,1)} %down_ref.1, bf16[384,1024]{1,0:T(8,128)(2,1)} %residual_ref.1, bf16[384,1024]{1,0:T(8,128)(2,1)} %early_ref.1, bf16[384,1024]{1,0:T(8,128)(2,1)} %middle_ref.1, bf16[3,1024,2560]{2,1,0:T(8,128)(2,1)} %merge_ref.1, ...), custom_call_target="tpu_custom_call" | custom-call | flops 34628173824 | bytes 90177536 | tf_op jit(solution)/shard_map/whole/pallas_call | solution.py:588
  169.3 2.1 %copy.14 = bf16[94,4096]{1,0:T(8,128)(2,1)} copy(bf16[94,4096]{1,0:T(8,128)(2,1)} %bitcast.3) | data formatting | bytes 1540096

commit v5 on v4

--- a/solution.py
+++ b/solution.py
@@ -89,7 +89,7 @@
     pl.semaphore_wait(barrier, 15)
 
 
-AHEAD = 3
+AHEAD = 4
 
 
 class Reduction:
@@ -456,60 +456,66 @@
 
     key = norm(merged_ref[4, :, :HS].astype(F32), k_gain_ref[...]).astype(BF)
     value = merged_ref[4, :, HS:]
-    for head in range(4):
-        lanes = slice(head % 2 * HS, head % 2 * HS + HS)
-        query = merged_ref[2 * core + head // 2, :, lanes].astype(F32)
-        query = norm(query, q_gain_ref[...]).astype(BF)
-        scores = lax.dot_general(
-            query, key, (((1,), (1,)), ((), ())), preferred_element_type=F32
-        ) / math.sqrt(HS)
-        scores = jnp.where(allowed, scores, -1e30)
-        expo = jnp.exp(scores - jnp.max(scores, axis=-1, keepdims=True))
-        weights = (expo / jnp.sum(expo, axis=-1, keepdims=True)).astype(BF)
-        result[:, head * HS : (head + 1) * HS] = matmul(weights, value).astype(BF)
-
-    padded, wide = slots.shape[1:]
-
-    def slot_copy(o, source):
-        columns = pl.ds(pl.multiple_of(source * wide, wide), wide)
+    padded, wide = slots.shape[2:]
+    source = 2 * z + core
+    which = lax.broadcasted_iota(jnp.int32, (padded, rows), 0)
+
+    def slot_columns(part, place):
+        return pl.ds(pl.multiple_of((2 * place + part) * wide, wide), wide)
+
+    def slot_copy(part, o, place):
         return pltpu.make_async_remote_copy(
-            slots.at[o], out_ref.at[:, columns], slot_send.at[o], slot_recv.at[source],
+            slots.at[part, o], out_ref.at[:, slot_columns(part, place)],
+            slot_send.at[part, o], slot_recv.at[part, place],
             device_id={"tensor": o, "dp": y}, device_id_type=MESH,
         )
 
-    source = 2 * z + core
-    which = lax.broadcasted_iota(jnp.int32, (padded, rows), 0)
-
-    def send(i, _):
-        o = (chip + 1 + i) % 8
-        hit = (which + o * capacity == slot) & (which < capacity)
-        slots[o] = matmul(jnp.where(hit, 1.0, 0.0).astype(BF), result[...]).astype(BF)
-        local = (o == chip) & (core == y)
-
-        @pl.when(local)
-        def _():
-            out_ref[:, pl.ds(pl.multiple_of(source * wide, wide), wide)] = slots[o]
-
-        @pl.when(jnp.logical_not(local))
-        def _():
-            slot_copy(o, source).start()
-
-        return 0
-
-    lax.fori_loop(0, 8, send, 0)
-
-    def close(i, _):
-        @pl.when(jnp.logical_not((i == chip) & (core == y)))
-        def _():
-            slot_copy(i, source).wait_send()
-
-        @pl.when(jnp.logical_not((i == source) & (core == y)))
-        def _():
-            slot_copy(chip, i).wait_recv()
-
-        return 0
-
-    lax.fori_loop(0, 8, close, 0)
+    for part in range(2):
+        for head in range(2):
+            lanes = slice(head * HS, (head + 1) * HS)
+            query = merged_ref[2 * core + part, :, lanes].astype(F32)
+            query = norm(query, q_gain_ref[...]).astype(BF)
+            scores = lax.dot_general(
+                query, key, (((1,), (1,)), ((), ())), preferred_element_type=F32
+            ) / math.sqrt(HS)
+            scores = jnp.where(allowed, scores, -1e30)
+            expo = jnp.exp(scores - jnp.max(scores, axis=-1, keepdims=True))
+            weights = (expo / jnp.sum(expo, axis=-1, keepdims=True)).astype(BF)
+            result[part, :, lanes] = matmul(weights, value).astype(BF)
+
+        def send(i, _):
+            o = (chip + 1 + i) % 8
+            hit = (which + o * capacity == slot) & (which < capacity)
+            hit = jnp.where(hit, 1.0, 0.0).astype(BF)
+            slots[part, o] = matmul(hit, result[part]).astype(BF)
+            local = (o == chip) & (core == y)
+
+            @pl.when(local)
+            def _():
+                out_ref[:, slot_columns(part, source)] = slots[part, o]
+
+            @pl.when(jnp.logical_not(local))
+            def _():
+                slot_copy(part, o, source).start()
+
+            return 0
+
+        lax.fori_loop(0, 8, send, 0)
+
+    for part in range(2):
+
+        def close(i, _):
+            @pl.when(jnp.logical_not((i == chip) & (core == y)))
+            def _():
+                slot_copy(part, i, source).wait_send()
+
+            @pl.when(jnp.logical_not((i == source) & (core == y)))
+            def _():
+                slot_copy(part, chip, i).wait_recv()
+
+            return 0
+
+        lax.fori_loop(0, 8, close, 0)
 
 
 def whole_kernel(
@@ -594,8 +600,8 @@
             pltpu.VMEM((3, 2 * rows, width), BF),
             pltpu.VMEM((5, rows, TILE), BF),
             pltpu.VMEM((2, 8, rows), jnp.int32),
-            pltpu.VMEM((rows, 4 * HS), BF),
-            pltpu.VMEM((8, padded, 4 * HS), BF),
+            pltpu.VMEM((2, rows, 2 * HS), BF),
+            pltpu.VMEM((2, 8, padded, 2 * HS), BF),
             pltpu.VMEM((2, rows, depth), BF),
             pltpu.VMEM((2, depth, TILE), BF),
             pltpu.VMEM((2, rows, width), BF),
@@ -608,7 +614,7 @@
             dma(2, 2),
             *unit_sems(count2),
             dma(count2), dma(count2),
-            dma(8), dma(8),
+            dma(2, 8), dma(2, 8),
         ],
         compiler_params=pltpu.CompilerParams(
             collective_id=0, has_side_effects=True, vmem_limit_bytes=60 << 20

time: 172 us -> 170 us (0.988)
  no operation moved by 1% of the time
where the time goes in v5:
time: 170 us
  Pallas kernels  167 us (98%)
  local copies, waits for them, and re-layouts  3.31 us (2%)
    pallas_call x1, Pallas kernels, grid_local(): pl.pallas_call(whole_kernel, out_shape=jax.ShapeDtypeStruct((padded, QH *...  167 us

profile of v5, /device:TPU:14, one launch (start us, length us, event | category | flops | bytes accessed | tf_op | source)
XLA Modules:
  0.0 169.9 jit_solution(5043508101125528740)
XLA Ops:
  0.0 1.2 reshape.11.mask_ref
  1.2 166.5 %whole.1 = bf16[96,4096]{1,0:T(8,128)(2,1)} custom-call(bf16[384,3584]{1,0:T(8,128)(2,1)} %hidden_ref.1, bf16[3584,4096]{1,0:T(8,128)(2,1)} %down_ref.1, bf16[384,1024]{1,0:T(8,128)(2,1)} %residual_ref.1, bf16[384,1024]{1,0:T(8,128)(2,1)} %early_ref.1, bf16[384,1024]{1,0:T(8,128)(2,1)} %middle_ref.1, bf16[3,1024,2560]{2,1,0:T(8,128)(2,1)} %merge_ref.1, ...), custom_call_target="tpu_custom_call" | custom-call | flops 34628173824 | bytes 90177536 | tf_op jit(solution)/shard_map/whole/pallas_call | solution.py:594
  167.8 2.1 %copy.14 = bf16[94,4096]{1,0:T(8,128)(2,1)} copy(bf16[94,4096]{1,0:T(8,128)(2,1)} %bitcast.3) | data formatting | bytes 1540096
